TPU v7x, 256 devices: a whole 4x4x8 slice. The times are simulated.
256 devices in a mesh: ctx: 32 (over y_hi, z, core), ch: 8 (over y_lo, x).
Axes of the slice: x: 4, y: 4 (y_hi: 2, y_lo: 2; y = y_hi * 2 + y_lo), z: 8, core: 2. Of those that a mesh axis runs over, the one named last changes fastest.
Arguments:
- projected: bfloat16 [3, 8192, 4096], P(None, 'ctx', 'ch'), may hold values from -6 to 6
- short_filter: float32 [3, 7, 4096], P(None, None, 'ch'), may hold values from -3 to 3
- residues: float32 [16, 4096], P(None, 'ch'), may hold values from -0.6 to 0.6
- decay_rates: float32 [16, 4096], P(None, 'ch'), may hold values from 0.0001 to 0.05
- doc_blocks: int32 [16], replicated, may hold values from 1 to 32, 64 in all
- out_weight: bfloat16 [4096, 4096], P('ctx', 'ch'), may hold values from -0.09375 to 0.09375
Outputs:
- mixed: bfloat16 [8192, 4096], P('ctx', 'ch')
Inputs may be any that keep to these rules, and one draw needn't show every extreme that they name: `doc_blocks`: each length counts blocks of 128 tokens; the lengths sum to 8192 // 128, and one sequence has exactly 32 blocks.
All inputs are finite; a program needn't handle non-finite values.
Results may differ from a plain program's by a relative error of at most 0.0049.
Values may be sent and summed in bfloat16 or wider, within the bound.
A program may use at most 64 MiB of HBM per device.

v0:
```python
import math

import jax
import jax.numpy as jnp
from jax import lax
from jax.sharding import PartitionSpec as P

ORDER = 16
SHORT = 7
BLK = 128


def passed_along(array, axis, by):
    size = lax.axis_size(axis)
    pairs = [(i, i + by) for i in range(size) if 0 <= i + by < size]
    return lax.ppermute(array, axis, pairs)


def carried_in(value, axis, join, neutral):
    count, mine = (lax.axis_size(axis), lax.axis_index(axis))
    pieces = jax.tree.map(lambda part: lax.all_gather(part, axis), value)
    total = jax.tree.map(
        lambda part, zero: jnp.full_like(part, 0) + jnp.asarray(zero, part.dtype), value, neutral
    )

    def lap(position, total):
        longer = join(total, jax.tree.map(lambda part: part[position], pieces))
        return jax.tree.map(lambda new, old: jnp.where(position < mine, new, old), longer, total)

    return lax.fori_loop(0, count - 1, lap, total)


def shards(projected, short_filter, residues, decay_rates, doc_blocks, out_weight):
    highest = lax.Precision.HIGHEST
    tok_rows = projected.shape[1]
    chans = projected.shape[2]
    blocks = tok_rows // BLK
    place = lax.axis_index("ctx")
    ends = jnp.cumsum(doc_blocks)
    starts_at = ends - doc_blocks
    block_ids = place * blocks + jnp.arange(blocks, dtype=jnp.int32)
    is_start = jnp.any(block_ids[:, None] == starts_at[None, :], axis=1)
    start_tok = jnp.repeat(is_start, BLK, total_repeat_length=tok_rows)
    within = jnp.arange(tok_rows, dtype=jnp.int32) % BLK
    rim = passed_along(projected[:, tok_rows - (SHORT - 1) :, :], "ctx", 1)
    extended = jnp.concatenate([rim, projected], axis=1).astype(jnp.float32)
    filtered = jnp.zeros((3, tok_rows, chans), jnp.float32)
    for tap in range(SHORT):
        keep = jnp.logical_or(within >= tap, jnp.logical_not(start_tok)).astype(jnp.float32)
        window = extended[:, SHORT - 1 - tap : SHORT - 1 - tap + tok_rows, :]
        filtered = filtered + short_filter[:, tap, None, :] * window * keep[None, :, None]
    query = filtered[0]
    source = filtered[1] * filtered[2]
    blocked = source.reshape(blocks, BLK, chans)
    span = 2 * BLK
    freq_ids = jnp.arange(span, dtype=jnp.int32)[:, None]
    pos_ids = jnp.arange(BLK, dtype=jnp.int32)[None, :]
    angles = (freq_ids * pos_ids % span).astype(jnp.float32) * (2.0 * math.pi / span)
    cos_tab = jnp.cos(angles)
    sin_tab = jnp.sin(angles)
    lags = jnp.arange(BLK, dtype=jnp.float32)
    head = jnp.sum(
        residues[:, None, :] * jnp.exp(-decay_rates[:, None, :] * lags[None, :, None]), axis=0
    )
    filt_re = jnp.dot(cos_tab, head, precision=highest)
    filt_im = -jnp.dot(sin_tab, head, precision=highest)
    spec_re = jnp.einsum("fn,jnc->jfc", cos_tab, blocked, precision=highest)
    spec_im = -jnp.einsum("fn,jnc->jfc", sin_tab, blocked, precision=highest)
    prod_re = spec_re * filt_re[None] - spec_im * filt_im[None]
    prod_im = spec_re * filt_im[None] + spec_im * filt_re[None]
    intra = (
        jnp.einsum("ft,jfc->jtc", cos_tab, prod_re, precision=highest)
        - jnp.einsum("ft,jfc->jtc", sin_tab, prod_im, precision=highest)
    ) * (1.0 / span)
    tail = jnp.exp(-decay_rates[:, None, :] * (BLK - 1 - lags)[None, :, None])
    own_end = jnp.einsum("rsc,jsc->jrc", tail, blocked, precision=highest)
    step_decay = jnp.exp(-decay_rates * BLK)

    def advance(carry, inputs):
        own, begin = inputs
        entering = jnp.where(begin, jnp.zeros_like(carry), carry)
        return (step_decay * entering + own, entering)

    zero_state = jnp.zeros((ORDER, chans), jnp.float32)
    final, entering_zero = lax.scan(advance, zero_state, (own_end, is_start))
    unbroken = jnp.cumprod(1.0 - is_start.astype(jnp.float32))
    steps_in = jnp.arange(blocks, dtype=jnp.float32)
    factors = jnp.exp(-decay_rates[None] * BLK * steps_in[:, None, None]) * unbroken[:, None, None]
    through = jnp.exp(-decay_rates * (BLK * blocks)) * unbroken[blocks - 1]

    def compose(earlier, later):
        return (earlier[0] * later[0], later[0] * earlier[1] + later[1])

    _, incoming = carried_in(
        (through, final), "ctx", compose, (jnp.ones((ORDER, chans), jnp.float32), zero_state)
    )
    states = entering_zero + factors * incoming[None]
    reach = residues[:, None, :] * jnp.exp(-decay_rates[:, None, :] * (lags + 1.0)[None, :, None])
    inter = jnp.einsum("rtc,jrc->jtc", reach, states, precision=highest)
    response = (intra + inter).reshape(tok_rows, chans)
    hidden = (query * response).astype(jnp.bfloat16)
    whole = lax.all_gather(hidden, "ch", axis=1, tiled=True)
    empty = jnp.zeros((tok_rows, out_weight.shape[1]), jnp.float32)
    piece = lax.all_gather(out_weight, "ctx", axis=0, tiled=True)
    columns = lax.slice_in_dim(whole, 0, piece.shape[0], axis=1)
    mixed = empty + jnp.dot(columns, piece, preferred_element_type=jnp.float32)
    return mixed.astype(jnp.bfloat16)


def solution(mesh):
    placed = (
        P(None, "ctx", "ch"),
        P(None, None, "ch"),
        P(None, "ch"),
        P(None, "ch"),
        P(),
        P("ctx", "ch"),
    )
    return jax.shard_map(
        shards, mesh=mesh, in_specs=placed, out_specs=P("ctx", "ch"), check_vma=False
    )
```

profile of v0, /device:TPU:1, one launch (start us, length us, event | category | flops | bytes accessed | tf_op | source)
XLA Modules:
  0.0 355.3 jit_solution(11078905698994371456)
XLA Ops:
  6.5 0.7 slice.75
  7.3 4.9 %collective-permute-start = (bf16[3,6,512]{2,1,0:T(8,128)(2,1)S(1)}, bf16[3,6,512]{2,1,0:T(8,128)(2,1)S(1)}, u32[]{:S(2)}, u32[]{:S(2)}) collective-permute-start(bf16[3,6,512]{2,1,0:T(8,128)(2,1)S(1)} %slice.75), channel_id=1, source_target_pairs={{0,8},{8,16},{16,24},{24,32},{32,40},{40,48},{48,56},{56,64},{64,7... | collective-permute-start | bytes 55304 | tf_op jit(solution)/shard_map/ppermute | solution.py:16
  12.2 0.7 copy.52
  14.7 2.0 broadcast_multiply_fusion
  17.5 1.4 select_reduce_fusion
  18.8 1.2 fusion.92
  20.3 1.4 maximum_convert_fusion
  21.7 2.2 fusion.14
  23.9 1.2 copy-done
  25.3 6.7 %fusion.30 = f32[2,16,512]{1,0,2:T(2,128)S(1)} fusion(f32[2,128,512]{1,0,2:T(2,128)S(1)} %copy.63, f32[128]{0:T(128)S(1)} %iota_subtract_fusion, f32[16,512]{0,1:T(8,128)S(1)} %copy.56), kind=kOutput, calls=%fused_computation.46 | convolution fusion | flops 26214400 | bytes 623104 | tf_op jit(solution)/shard_map/rsc,jsc->jrc/dot_general | solution.py:76
  32.3 4.2 %while.28 = (s32[]{:T(128)}, f32[16,512]{1,0:T(8,128)S(1)}, f32[2,16,512]{2,1,0:T(8,128)S(1)}, pred[2]{0:T(512)(128)(4,1)S(1)}, f32[16,512]{1,0:T(8,128)S(1)}, /...) while((s32[]{:T(128)}, f32[16,512]{1,0:T(8,128)S(1)}, f32[2,16,512]{2,1,0:T(8,128)S(1)}, ...), condition=%wide.region_4.5_spmd.clone, body=%wide.region_3.4_spmd.clone.sunk | while | flops 49155 | bytes 196720 | solution.py:85
  32.3 0.7 dynamic_slice.34
  32.9 0.7 bitcast_dynamic-update-slice_fusion.2
  33.6 0.7 bitcast_add_fusion.3
  35.0 0.7 bitcast_dynamic-update-slice_fusion.2
  35.7 0.7 bitcast_add_fusion.3
  37.3 6.1 %multiply_reduce_fusion = f32[128,512]{0,1:T(8,128)S(1)} fusion(f32[16,512]{0,1:T(8,128)S(1)} %copy.56, f32[16,512]{0,1:T(8,128)S(1)} %copy.55), kind=kLoop, calls=%fused_computation.13 | loop fusion | flops 3080192 | bytes 327680 | tf_op jit(solution)/shard_map/reduce_sum | solution.py:62
  43.4 1.1 convolution_negate_fusion.1
  44.8 1.1 fusion.59
  45.9 1.5 convolution_bitcast_fusion
  47.3 1.5 fusion.26
  48.8 2.6 fusion.36
  51.4 45.1 %all-gather.11.cloned.1.call-done = f32[512,512]{1,0:T(8,128)} async-done(((f32[16,512]{1,0:T(8,128)}), f32[512,512]{1,0:T(8,128)}) %all-gather.11.cloned.1.call-update) | async-done | bytes 1048592 | tf_op jit(solution)/shard_map/all_gather | solution.py:21
  96.5 77.2 %all-gather.13.cloned.1.call-done = f32[512,512]{1,0:T(8,128)} async-done(((f32[16,512]{1,0:T(8,128)}), f32[512,512]{1,0:T(8,128)}) %all-gather.13.cloned.1.call-update) | async-done | bytes 1048592 | tf_op jit(solution)/shard_map/all_gather | solution.py:21
  173.7 25.2 %while.29 = (s32[]{:T(128)}, f32[16,512]{1,0:T(8,128)S(1)}, s32[]{:T(128)}, f32[32,16,512]{2,1,0:T(8,128)}, f32[32,16,512]{2,1,0:T(8,128)}, /*index=5*/s32[]{:T(128)}, s32[]{:T(128)}) while((s32[]{:T(128)}, f32[16,512]{1,0:T(8,128)S(1)}, s32[]{:T(128)}, f32[32,16,512]{2,1,0:T(8,128)}, f32[32,16,512]{2,1,0:T(8,128)}, ...), condition=%wide.region_7.8_spmd.clone, body=%wide.region_6.7_spmd.clone.sunk | while | flops 32772 | bytes 131173 | solution.py:30
  173.7 0.8 fusion.103
  174.5 0.8 fusion.103
  175.3 0.8 fusion.103
  176.1 0.8 fusion.103
  176.9 0.8 fusion.103
  177.7 0.8 fusion.103
  178.5 0.8 fusion.103
  179.4 0.8 fusion.103
  180.2 0.8 fusion.103
  181.0 0.8 fusion.103
  181.8 0.8 fusion.103
  182.6 0.8 fusion.103
  183.4 0.8 fusion.103
  184.2 0.8 fusion.103
  185.1 0.8 fusion.103
  185.9 0.8 fusion.103
  186.7 0.8 fusion.103
  187.5 0.8 fusion.103
  188.3 0.8 fusion.103
  189.1 0.8 fusion.103
  189.9 0.8 fusion.103
  190.7 0.8 fusion.103
  191.6 0.8 fusion.103
  192.4 0.8 fusion.103
  193.2 0.8 fusion.103
  194.0 0.8 fusion.103
  194.8 0.8 fusion.103
  195.6 0.8 fusion.103
  196.4 0.8 fusion.103
  197.2 0.8 fusion.103
  198.1 0.8 fusion.103
  199.0 1.0 copy.65
  200.0 7.2 %fusion.1 = f32[512,2,128]{2,1,0:T(2,128)} fusion(f32[2,16,512]{1,0,2:T(2,128)} %copy.65, f32[128]{0:T(128)S(1)} %iota_add_fusion.1, f32[16,512]{0,1:T(8,128)S(1)} %copy.56, f32[16,512]{0,1:T(8,128)} %copy-done.4), kind=kOutput, calls=%fused_computation.6 | convolution fusion | flops 27262976 | bytes 655872 | tf_op jit(solution)/shard_map/rtc,jrc->jtc/dot_general | solution.py:99
  207.2 2.0 copy.66
  209.2 3.0 fusion.29
  212.3 1.8 fusion.41
  214.7 35.2 %all-gather.7.cloned.1.call-done = bf16[256,4096]{1,0:T(8,128)(2,1)} async-done(((bf16[256,512]{1,0:T(8,128)(2,1)}), bf16[256,4096]{1,0:T(8,128)(2,1)}) %all-gather.7.cloned.1.call-update) | async-done | bytes 2097168 | tf_op jit(solution)/shard_map/all_gather | solution.py:102
  249.9 94.1 %all-gather.9.cloned.1.call-done = bf16[4096,512]{1,0:T(8,128)(2,1)} async-done(((bf16[128,512]{1,0:T(8,128)(2,1)}), bf16[4096,512]{1,0:T(8,128)(2,1)}) %all-gather.9.cloned.1.call-update) | async-done | bytes 4194320 | tf_op jit(solution)/shard_map/all_gather | solution.py:104
  344.0 4.8 %convolution_convert_fusion = bf16[256,512]{1,0:T(8,128)(2,1)} fusion(bf16[256,4096]{1,0:T(8,128)(2,1)} %all-gather.7.cloned.1.call-done, bf16[4096,512]{1,0:T(8,128)(2,1)} %all-gather.9.cloned.1.call-done), kind=kOutput, calls=%fused_computation.48 | convolution fusion | flops 1073872896 | bytes 6553600 | tf_op jit(solution)/shard_map/dot_general | solution.py:106
  (54 shorter events, 5.4 us)
Async XLA Ops:
  6.5 90.0 %all-gather.11.cloned.1.call-start = ((), (), s32[]{:S(2)}) async-start(), calls=%async_computation.2 | async-start | bytes 1081344 | tf_op jit(solution)/shard_map/all_gather | solution.py:21
  7.3 13.0 %collective-permute-start = (bf16[3,6,512]{2,1,0:T(8,128)(2,1)S(1)}, bf16[3,6,512]{2,1,0:T(8,128)(2,1)S(1)}, u32[]{:S(2)}, u32[]{:S(2)}) collective-permute-start(bf16[3,6,512]{2,1,0:T(8,128)(2,1)S(1)} %slice.75), channel_id=1, source_target_pairs={{0,8},{8,16},{16,24},{24,32},{32,40},{40,48},{48,56},{56,64},{64,7... | collective-permute-start | bytes 55304 | tf_op jit(solution)/shard_map/ppermute | solution.py:16
  16.8 156.9 %all-gather.13.cloned.1.call-start = ((), (), s32[]{:S(2)}) async-start(), calls=%async_computation.3 | async-start | bytes 1081344 | tf_op jit(solution)/shard_map/all_gather | solution.py:21
  23.9 1.2 copy-start
  32.1 5.0 %copy-start.7 = (f32[16,512]{1,0:T(8,128)S(1)}, f32[16,512]{1,0:T(8,128)}, u32[]{:S(2)}) copy-start(f32[16,512]{1,0:T(8,128)} %param.14) | copy-start | bytes 98308
  36.4 0.6 copy-start.3
  36.4 0.8 copy-start.5
  37.1 212.9 %all-gather.7.cloned.1.call-start = ((), (), s32[]{:S(2)}) async-start(), calls=%async_computation | async-start | bytes 2359296 | tf_op jit(solution)/shard_map/all_gather | solution.py:102
  37.3 6.2 %copy-start.4 = (f32[16,512]{0,1:T(8,128)}, f32[16,512]{0,1:T(8,128)S(1)}, u32[]{:S(2)}) copy-start(f32[16,512]{0,1:T(8,128)S(1)} %copy.55) | copy-start | bytes 98308
  45.8 3.0 copy-start.1
  48.8 150.0 %copy-start.6 = (f32[2,16,512]{2,1,0:T(8,128)S(1)}, f32[2,16,512]{2,1,0:T(8,128)}, u32[]{:S(2)}) copy-start(f32[2,16,512]{2,1,0:T(8,128)} %copy-done.5) | copy-start | bytes 196612
  200.0 9.3 %copy-start.2 = (f32[256,512]{0,1:T(8,128)S(1)}, f32[256,512]{0,1:T(8,128)}, u32[]{:S(2)}) copy-start(f32[256,512]{0,1:T(8,128)} %copy-done.1) | copy-start | bytes 1572868
  214.1 129.9 %all-gather.9.cloned.1.call-start = ((), (), s32[]{:S(2)}) async-start(), calls=%async_computation.1 | async-start | bytes 4325376 | tf_op jit(solution)/shard_map/all_gather | solution.py:104
Sparse Core Ops, SparseCore 0:
  16.9 79.5 all-gather.10
  99.3 74.3 all-gather.12
  214.2 35.6 all-gather.6
  252.5 91.3 all-gather.8
where the time goes:
time: 358 us; the launch traced here: 355 us
  waiting for transfers between devices  252 us (70%)
  other arithmetic  43.5 us (12%)
  matrix products  29.5 us (8%)
  between operations  13.5 us (4%)
  local copies, waits for them, and re-layouts  10.9 us (3%)
  starting transfers between devices  5.06 us (1%)
    all_gather x2, waiting for transfers between devices, carried_in(): pieces = jax.tree.map(lambda part: lax.all_gather(part, axis), value)  122 us
    all_gather x1, waiting for transfers between devices, shards(): piece = lax.all_gather(out_weight, 'ctx', axis=0, tiled=True)  94.1 us
    all_gather x1, waiting for transfers between devices, shards(): whole = lax.all_gather(hidden, 'ch', axis=1, tiled=True)  35.2 us
    select_n x31, other arithmetic, lap(): jnp.where(position < mine, new, old)  24.5 us
    dot_general x1, matrix products, shards(): inter = jnp.einsum('rtc,jrc->jtc', reach, states, precision=highest)  7.23 us
  transfers between devices with their start and end apart: 5, of which 4 were waited for; matrix products, arithmetic and copies ran while one was open for 10% of the time, Pallas kernels for 0%

commit v1 on v0

v1 whole, which is shorter than its diff:
```python
import functools

import jax
import jax.numpy as jnp
import ml_dtypes
import numpy as np
from jax import lax
from jax.experimental import pallas as pl
from jax.experimental.pallas import tpu as pltpu
from jax.sharding import PartitionSpec as P

ORDER = 16
SHORT = 7
BLK = 128
LANES = 128
MESH = pl.DeviceIdType.MESH
F32, BF16 = jnp.float32, jnp.bfloat16


def dft_tables():
    freq = np.arange(BLK)[:, None] + 0.5
    angles = 2.0 * np.pi * freq * np.arange(BLK)[None, :] / (2 * BLK)
    table = np.concatenate([np.cos(angles), np.sin(angles)], axis=0)

    def split(a):
        high = a.astype(ml_dtypes.bfloat16)
        low = (a - high.astype(np.float64)).astype(ml_dtypes.bfloat16)
        return np.concatenate([high, high, low], axis=1)

    return split(table), split(table.T)


def split_rows(a):
    high = a.astype(BF16)
    low = (a - high.astype(F32)).astype(BF16)
    return jnp.concatenate([high, low, high], axis=0)


def kernel(
    proj, sf, res, dec, docs, w, fwd, inv, out,
    halo, ext, query, source, spec, intra, head, hspec,
    parts, rx, back, rx2, dparts, through, state, ends_own,
    wbuf, hbuf, acc,
    halo_sem, a2a_sem, ws, wr, hs, hr,
):
    p, q = lax.axis_index("ctx"), lax.axis_index("ch")
    n_ctx = lax.axis_size("ctx")
    core = p % 2
    z = (p // 2) % 8
    y_hi = p // 16
    x, y_lo = q % 4, q // 4

    def ctx_of(hi, zz, cc):
        return hi * 16 + zz * 2 + cc

    q_right = y_lo * 4 + (x + 1) % 4
    q_left = y_lo * 4 + (x + 3) % 4
    q_opp = y_lo * 4 + (x + 2) % 4
    q_y = (1 - y_lo) * 4 + x
    q_yright = (1 - y_lo) * 4 + (x + 1) % 4
    q_yleft = (1 - y_lo) * 4 + (x + 3) % 4
    q_yopp = (1 - y_lo) * 4 + (x + 2) % 4

    def remote(src, dst, send, recv, to_ctx, to_ch):
        return pltpu.make_async_remote_copy(
            src_ref=src, dst_ref=dst, send_sem=send, recv_sem=recv,
            device_id=(to_ctx, to_ch), device_id_type=MESH,
        )

    barrier = pltpu.get_barrier_semaphore()

    def greet(o, carry):
        pl.semaphore_signal(barrier, inc=1, device_id=((p + o) % n_ctx, q), device_id_type=MESH)
        return carry

    lax.fori_loop(1, n_ctx, greet, 0)
    for to in (q_right, q_left, q_y):
        pl.semaphore_signal(barrier, inc=1, device_id=(p, to), device_id_type=MESH)
    pl.semaphore_wait(barrier, n_ctx - 1 + 3)

    halo_copy = remote(
        proj.at[:, pl.ds(240, 16), :], halo, halo_sem.at[0], halo_sem.at[1], (p + 1) % n_ctx, q
    )
    halo_copy.start()

    step = 1 - 2 * core
    z_next = (z + step + 8) % 8
    hi_of = (y_hi, 1 - y_hi)
    sends = []

    def started(copy):
        copy.start()
        sends.append(copy)

    def half(hi, zz, cc):
        return wbuf.at[hi, zz, pl.ds(cc * 128, 128), :]

    def spread(plane, src):
        hi = hi_of[plane]
        dst = half(hi, z, core)
        started(remote(src, dst, ws.at[plane, 1], wr.at[plane, 1 + core], ctx_of(y_hi, (z + 1) % 8, 0), q))
        started(remote(src, dst, ws.at[plane, 2], wr.at[plane, 1 + core], ctx_of(y_hi, (z + 7) % 8, 1), q))
        started(remote(src, dst, ws.at[plane, 6], wr.at[plane, 6], ctx_of(y_hi, z, 1 - core), q))

    def landed(ref, sem):
        pltpu.make_async_copy(ref, ref, sem).wait()

    def pass_on(plane, hop):
        hi = hi_of[plane]
        oz = (z - step * hop + 8) % 8
        whole = wbuf.at[hi, oz]
        mine = half(hi, oz, core)
        if hop == 1:
            landed(half(hi, oz, 0), wr.at[plane, 1])
            landed(half(hi, oz, 1), wr.at[plane, 2])
        elif hop < 4:
            landed(whole, wr.at[plane, 1 + hop])
        else:
            landed(mine, wr.at[plane, 5])
        if hop < 3:
            started(remote(whole, whole, ws.at[plane, 2 + hop], wr.at[plane, 2 + hop], ctx_of(y_hi, z_next, core), q))
        elif hop == 3:
            started(remote(mine, mine, ws.at[plane, 5], wr.at[plane, 5], ctx_of(y_hi, z_next, core), q))
        part = whole if hop < 4 else mine
        started(remote(part, part, ws.at[plane, 6 + hop], wr.at[plane, 6 + hop], ctx_of(y_hi, z, 1 - core), q))

    spread(0, w)
    started(
        remote(w, half(y_hi, z, core), ws.at[1, 0], wr.at[1, 0], ctx_of(1 - y_hi, z, core), q)
    )
    half(y_hi, z, core)[...] = w[...]

    begins0, begins1, at = jnp.float32(0), jnp.float32(0), jnp.int32(0)
    rows = lax.broadcasted_iota(jnp.int32, (32, LANES), 0)
    unbroken = jnp.ones((32, LANES), F32)
    for n in range(docs.shape[0]):
        begins0 = jnp.where(at == 2 * p, 1.0, begins0)
        begins1 = jnp.where(at == 2 * p + 1, 1.0, begins1)
        unbroken = jnp.where(rows == at // 2, 0.0, unbroken)
        at = at + docs[n]
    goes0, goes1 = 1.0 - begins0, 1.0 - begins1

    tiles = proj.shape[2] // LANES
    sub = lax.broadcasted_iota(jnp.int32, (ORDER, 8, LANES), 1).astype(F32)

    def lane(t):
        return pl.ds(pl.multiple_of(t * LANES, LANES), LANES)

    def head_tile(t, carry):
        d = dec[:, lane(t)]
        lam8 = jnp.exp(-8.0 * d)[:, None, :]
        v = res[:, lane(t)][:, None, :] * jnp.exp(-d[:, None, :] * sub)
        pieces = []
        for k in range(BLK // 8):
            pieces.append(jnp.sum(v, axis=0))
            v = v * lam8
        head[:, lane(t)] = jnp.concatenate(pieces, axis=0)
        for i in range(8):
            dparts[i * tiles + t] = d[2 * i : 2 * i + 2]
        return carry

    lax.fori_loop(0, tiles, head_tile, 0)
    hspec[...] = jnp.dot(fwd[...], split_rows(head[...]), preferred_element_type=F32) * (1.0 / BLK)
    lam256 = jnp.exp(-256.0 * dparts[p])
    for n in range(32):
        through[n] = lam256 * unbroken[n : n + 1, :]

    halo_copy.wait()
    for s in range(3):
        for j in range(2):
            if j == 0:
                before = halo[s, :, :].astype(F32)[8:16]
                before = jnp.where(goes0 > 0.5, before, 0.0)
            else:
                before = proj[s, 112:128, :].astype(F32)[8:16]
                before = jnp.where(goes1 > 0.5, before, 0.0)
            ext[s, j, 0:8, :] = before
            ext[s, j, 8:136, :] = proj[s, j * BLK : (j + 1) * BLK, :].astype(F32)

    def short_tile(t, carry):
        for j in range(2):
            short = []
            for s in range(3):
                total = jnp.zeros((BLK, LANES), F32)
                for tap in range(SHORT):
                    total = total + sf[s, tap : tap + 1, lane(t)] * ext[s, j, 8 - tap : 136 - tap, lane(t)]
                short.append(total)
            query[j, :, lane(t)] = short[0]
            source[:, pl.ds(pl.multiple_of(j * tiles * LANES + t * LANES, LANES), LANES)] = short[1] * short[2]
        return carry

    lax.fori_loop(0, tiles, short_tile, 0)

    def end_tile(t, carry):
        d = dec[:, lane(t)]
        lam8 = jnp.exp(-8.0 * d)[:, None, :]
        lam128 = jnp.exp(-128.0 * d)
        weight = jnp.exp(-d[:, None, :] * (7.0 - sub))
        own = []
        for j in range(2):
            lanes = pl.ds(pl.multiple_of(j * tiles * LANES + t * LANES, LANES), LANES)
            total = jnp.zeros((ORDER, 8, LANES), F32)
            for k in range(BLK // 8):
                total = total * lam8 + source[8 * k : 8 * k + 8, lanes][None]
            own.append(jnp.sum(total * weight, axis=1))
        ends_own[:, lane(t)] = own[0]
        final = own[1] + lam128 * own[0] * goes1
        for i in range(8):
            parts[i * tiles + t] = final[2 * i : 2 * i + 2]
        return carry

    lax.fori_loop(0, tiles, end_tile, 0)

    def to_all(src, dst, send, recv):
        def one(o, carry):
            to = (p + o) % n_ctx
            remote(src.at[to], dst.at[p], send, recv, to, q).start()
            return carry

        lax.fori_loop(1, n_ctx, one, 0)
        dst[p] = src[p]

    def all_in(buf, sem):
        landed(buf.at[pl.ds(0, 31)], sem)

    to_all(parts, rx, a2a_sem.at[0], a2a_sem.at[1])
    pass_on(0, 1)
    seed = half(1 - y_hi, z, core)
    landed(seed, wr.at[1, 0])
    spread(1, seed)
    spec[...] = jnp.dot(fwd[...], split_rows(source[...]), preferred_element_type=F32)
    all_in(rx, a2a_sem.at[1])

    def scan(n, s):
        back[n] = s
        return s * through[n] + rx[n]

    lax.fori_loop(0, 32, scan, jnp.zeros((2, LANES), F32))
    to_all(back, rx2, a2a_sem.at[2], a2a_sem.at[3])
    pass_on(0, 2)

    chans = proj.shape[2]
    for j in range(2):
        cols = slice(j * chans, (j + 1) * chans)
        s_re, s_im = spec[0:BLK, cols], spec[BLK : 2 * BLK, cols]
        h_re, h_im = hspec[0:BLK, :], hspec[BLK : 2 * BLK, :]
        y_re = s_re * h_re - s_im * h_im
        y_im = s_re * h_im + s_im * h_re
        both = jnp.concatenate([y_re, y_im], axis=0)
        intra[j] = jnp.dot(inv[...], split_rows(both), preferred_element_type=F32)
    pass_on(1, 1)

    all_in(rx2, a2a_sem.at[3])
    for t in range(tiles):
        for i in range(8):
            state[2 * i : 2 * i + 2, t * LANES : (t + 1) * LANES] = rx2[i * tiles + t]

    def hidden_block(j):
        def hidden_tile(t, carry):
            d = dec[:, lane(t)]
            lam8 = jnp.exp(-8.0 * d)[:, None, :]
            entering = state[:, lane(t)] * goes0
            if j == 1:
                entering = (jnp.exp(-128.0 * d) * entering + ends_own[:, lane(t)]) * goes1
            v = (res[:, lane(t)] * entering)[:, None, :] * jnp.exp(-d[:, None, :] * (sub + 1.0))
            pieces = []
            for k in range(BLK // 8):
                pieces.append(jnp.sum(v, axis=0))
                v = v * lam8
            response = intra[j, :, lane(t)] + jnp.concatenate(pieces, axis=0)
            hbuf[q, j * BLK : (j + 1) * BLK, lane(t)] = (query[j, :, lane(t)] * response).astype(BF16)
            return carry

        lax.fori_loop(0, tiles, hidden_tile, 0)

    def piece(b, j):
        return hbuf.at[b, pl.ds(j * BLK, BLK), :]

    def give(idx, b, j, to):
        started(remote(piece(b, j), piece(b, j), hs.at[idx], hr.at[idx], p, to))

    def took(idx, b, j):
        landed(piece(b, j), hr.at[idx])

    for j in range(2):
        hidden_block(j)
        give(0 + j, q, j, q_right)
        give(2 + j, q, j, q_left)
        give(4 + j, q, j, q_y)
    pass_on(0, 3)
    pass_on(1, 2)
    took(0, q_left, 0)
    give(6, q_left, 0, q_right)
    give(8, q_left, 0, q_y)
    took(2, q_right, 0)
    give(9, q_right, 0, q_y)
    took(3, q_right, 1)
    give(7, q_right, 1, q_left)
    took(5, q_y, 1)
    give(10, q_y, 1, q_right)
    give(11, q_y, 1, q_left)
    pass_on(0, 4)
    pass_on(1, 3)
    took(8, q_yleft, 0)
    give(12, q_yleft, 0, q_right)
    took(11, q_yright, 1)
    give(13, q_yright, 1, q_left)
    pass_on(1, 4)

    for plane in range(2):
        hi = hi_of[plane]
        landed(half(hi, z, 1 - core), wr.at[plane, 6])
        for hop in range(1, 5):
            oz = (z + step * hop + 8) % 8
            landed(wbuf.at[hi, oz] if hop < 4 else half(hi, oz, 1 - core), wr.at[plane, 6 + hop])
    took(1, q_left, 1)
    took(4, q_y, 0)
    took(6, q_opp, 0)
    took(7, q_opp, 1)
    took(9, q_yright, 0)
    took(10, q_yleft, 1)

    acc[...] = jnp.zeros_like(acc)

    def project(k, carry):
        m = k % 4
        dx = m + (m // 2) * (1 - 2 * (m % 2))
        b = ((y_lo + k // 4) % 2) * 4 + (x + dx) % 4
        weights = wbuf[b // 4, pl.ds(2 * (b % 4), 2)].reshape(4 * BLK, acc.shape[1])
        acc[...] += jnp.dot(hbuf[b], weights, preferred_element_type=F32)
        return carry

    lax.fori_loop(0, 7, project, 0)
    took(12, q_yopp, 0)
    took(13, q_yopp, 1)
    lax.fori_loop(7, 8, project, 0)
    out[...] = acc[...].astype(BF16)

    for copy in sends:
        copy.wait_send()
    landed(parts.at[pl.ds(0, 31)], a2a_sem.at[0])
    landed(back.at[pl.ds(0, 31)], a2a_sem.at[2])


def shards(fwd, inv, projected, short_filter, residues, decay_rates, doc_blocks, out_weight):
    rows, chans = projected.shape[1:]
    vmem = pl.BlockSpec(memory_space=pltpu.VMEM)
    return pl.pallas_call(
        kernel,
        out_shape=jax.ShapeDtypeStruct((rows, out_weight.shape[1]), BF16),
        in_specs=[vmem] * 4 + [pl.BlockSpec(memory_space=pltpu.SMEM)] + [vmem] * 3,
        out_specs=vmem,
        scratch_shapes=[
            pltpu.VMEM((3, 16, chans), BF16),
            pltpu.VMEM((3, 2, 8 + BLK, chans), F32),
            pltpu.VMEM((2, BLK, chans), F32),
            pltpu.VMEM((BLK, 2 * chans), F32),
            pltpu.VMEM((2 * BLK, 2 * chans), F32),
            pltpu.VMEM((2, BLK, chans), F32),
            pltpu.VMEM((BLK, chans), F32),
            pltpu.VMEM((2 * BLK, chans), F32),
            pltpu.VMEM((32, 2, LANES), F32),
            pltpu.VMEM((32, 2, LANES), F32),
            pltpu.VMEM((32, 2, LANES), F32),
            pltpu.VMEM((32, 2, LANES), F32),
            pltpu.VMEM((32, 2, LANES), F32),
            pltpu.VMEM((32, 2, LANES), F32),
            pltpu.VMEM((ORDER, chans), F32),
            pltpu.VMEM((ORDER, chans), F32),
            pltpu.VMEM((2, 8, 2 * BLK, out_weight.shape[1]), BF16),
            pltpu.VMEM((8, rows, chans), BF16),
            pltpu.VMEM((rows, out_weight.shape[1]), F32),
            pltpu.SemaphoreType.DMA((2,)),
            pltpu.SemaphoreType.DMA((4,)),
            pltpu.SemaphoreType.DMA((2, 11)),
            pltpu.SemaphoreType.DMA((2, 11)),
            pltpu.SemaphoreType.DMA((14,)),
            pltpu.SemaphoreType.DMA((14,)),
        ],
        compiler_params=pltpu.CompilerParams(
            collective_id=0, has_side_effects=True, vmem_limit_bytes=40 * 1024 * 1024
        ),
        name="hyena_block",
    )(projected, short_filter, residues, decay_rates, doc_blocks, out_weight, fwd, inv)


def solution(mesh):
    placed = (
        P(None, "ctx", "ch"),
        P(None, None, "ch"),
        P(None, "ch"),
        P(None, "ch"),
        P(),
        P("ctx", "ch"),
    )
    fwd, inv = (jnp.asarray(t) for t in dft_tables())
    return jax.shard_map(
        functools.partial(shards, fwd, inv), mesh=mesh, in_specs=placed, out_specs=P("ctx", "ch"), check_vma=False
    )
```

time: 358 us -> 57.5 us (0.16)
  waiting for transfers between devices: 252 us -> 0 us
  Pallas kernels: 0 us -> 49.6 us
  other arithmetic: 43.5 us -> 0 us
  matrix products: 29.5 us -> 0 us
  between operations: 13.5 us -> 0.02 us
  starting transfers between devices: 5.06 us -> 0 us
    all_gather x4 -> x0, waiting for transfers between devices: 252 us -> none  [the longest x2 122 us: carried_in(): pieces = jax.tree.map(lambda part: lax.all_gather(part, axis), value)]
    pallas_call x0 -> x1, Pallas kernels: none -> 49.6 us  [shards(): pl.pallas_call(kernel, out_shape=jax.ShapeDtypeStruct((rows, out_weight.s...]
    dot_general x9 -> x0, matrix products: 29.5 us -> none  [the longest x1 7.23 us: shards(): inter = jnp.einsum('rtc,jrc->jtc', reach, states, precision=highest)]
    select_n x31 -> x0, other arithmetic: 24.5 us -> none  [lap(): jnp.where(position < mine, new, old)]
    reduce_sum x1 -> x0, other arithmetic: 6.15 us -> none  [shards(): jnp.sum(residues[:, None, :] * jnp.exp(-decay_rates[:, None, :] * lags[No...]
    unnamed x22 -> x17, local copies, waits for them, and re-layouts: 2.08 us -> 7.56 us
    ppermute x1 -> x0, starting transfers between devices: 4.93 us -> none  [passed_along(): return lax.ppermute(array, axis, pairs)]
    add x7 -> x0, other arithmetic: 3.68 us -> none  [the longest x1 2.19 us: shards(): filtered + short_filter[:, tap, None, :] * window * keep[None, :, None]]
  transfers between devices with their start and end apart: 5 -> 0, of which waited for: 4 -> 0; matrix products, arithmetic and copies ran while one was open for 10% -> 0% of each run, Pallas kernels for 0% -> 0%
where the time goes in v1:
time: 57.5 us; the launch traced here: 57.1 us
  Pallas kernels  49.6 us (86%)
  local copies, waits for them, and re-layouts  7.56 us (13%)
    pallas_call x1, Pallas kernels, shards(): pl.pallas_call(kernel, out_shape=jax.ShapeDtypeStruct((rows, out_weight.s...  49.6 us
    unnamed x17, local copies, waits for them, and re-layouts  7.56 us

profile of v1, /device:TPU:1, one launch (start us, length us, event | category | flops | bytes accessed | tf_op | source)
XLA Modules:
  0.0 57.1 jit_solution(315987627162541797)
XLA Ops:
  0.0 0.0 copy-start
  0.0 1.1 %copy-done = bf16[3,256,512]{2,1,0:T(8,128)(2,1)S(1)} copy-done((bf16[3,256,512]{2,1,0:T(8,128)(2,1)S(1)}, bf16[3,256,512]{2,1,0:T(8,128)(2,1)}, u32[]{:S(2)}) %copy-start) | copy-done | bytes 786456
  1.1 0.0 copy-start.1
  1.1 0.9 %copy-done.1 = bf16[128,768]{1,0:T(8,128)(2,1)S(1)} copy-done((bf16[128,768]{1,0:T(8,128)(2,1)S(1)}, bf16[128,768]{1,0:T(8,128)(2,1)}, u32[]{:S(2)}) %copy-start.1) | copy-done | bytes 196632
  2.1 0.0 copy-start.2
  2.1 0.9 %copy-done.2 = bf16[256,384]{1,0:T(8,128)(2,1)S(1)} copy-done((bf16[256,384]{1,0:T(8,128)(2,1)S(1)}, bf16[256,384]{1,0:T(8,128)(2,1)}, u32[]{:S(2)}) %copy-start.2) | copy-done | bytes 196632
  3.0 0.0 copy-start.3
  3.0 0.9 %copy-done.3 = bf16[128,512]{1,0:T(8,128)(2,1)S(1)} copy-done((bf16[128,512]{1,0:T(8,128)(2,1)S(1)}, bf16[128,512]{1,0:T(8,128)(2,1)}, u32[]{:S(2)}) %copy-start.3) | copy-done | bytes 131096
  3.9 0.0 copy-start.4
  3.9 0.8 %copy-done.4 = f32[3,7,512]{2,1,0:T(8,128)S(1)} copy-done((f32[3,7,512]{2,1,0:T(8,128)S(1)}, f32[3,7,512]{2,1,0:T(8,128)}, u32[]{:S(2)}) %copy-start.4) | copy-done | bytes 43032
  4.7 0.0 copy-start.5
  4.7 0.8 %copy-done.5 = f32[16,512]{1,0:T(8,128)S(1)} copy-done((f32[16,512]{1,0:T(8,128)S(1)}, f32[16,512]{1,0:T(8,128)}, u32[]{:S(2)}) %copy-start.5) | copy-done | bytes 32792
  5.5 0.0 copy-start.6
  5.5 0.8 %copy-done.6 = f32[16,512]{1,0:T(8,128)S(1)} copy-done((f32[16,512]{1,0:T(8,128)S(1)}, f32[16,512]{1,0:T(8,128)}, u32[]{:S(2)}) %copy-start.6) | copy-done | bytes 32792
  6.2 0.0 copy-start.7
  6.2 0.7 %copy-done.7 = s32[16]{0:T(128)S(1)} copy-done((s32[16]{0:T(128)S(1)}, s32[16]{0:T(128)}, u32[]{:S(2)}) %copy-start.7) | copy-done | bytes 88
  6.9 49.6 %hyena_block.1 = bf16[256,512]{1,0:T(8,128)(2,1)S(1)} custom-call(bf16[3,256,512]{2,1,0:T(8,128)(2,1)S(1)} %copy-done, f32[3,7,512]{2,1,0:T(8,128)S(1)} %copy-done.4, f32[16,512]{1,0:T(8,128)S(1)} %copy-done.5, f32[16,512]{1,0:T(8,128)S(1)} %copy-done.6, s32[16]{0:T(128)S(1)} %copy-done.7, bf16[128,512]{1,0:T(8,128)(2,1)S(1)} %copy-done.3, ...), custom_call_target="tpu_custom_call" | custom-call | tf_op jit(solution)/shard_map/hyena_block/pallas_call | solution.py:348
  56.4 0.7 %copy.10 = bf16[256,512]{1,0:T(8,128)(2,1)} copy(bf16[256,512]{1,0:T(8,128)(2,1)S(1)} %hyena_block.1) | data formatting | bytes 524288
Async XLA Ops:
  0.0 1.1 %copy-start = (bf16[3,256,512]{2,1,0:T(8,128)(2,1)S(1)}, bf16[3,256,512]{2,1,0:T(8,128)(2,1)}, u32[]{:S(2)}) copy-start(bf16[3,256,512]{2,1,0:T(8,128)(2,1)} %proj.1) | copy-start | bytes 2359300
  1.1 0.9 %copy-start.1 = (bf16[128,768]{1,0:T(8,128)(2,1)S(1)}, bf16[128,768]{1,0:T(8,128)(2,1)}, u32[]{:S(2)}) copy-start(bf16[128,768]{1,0:T(8,128)(2,1)} %constant.5.clone.inv) | copy-start | bytes 589828
  2.1 0.9 %copy-start.2 = (bf16[256,384]{1,0:T(8,128)(2,1)S(1)}, bf16[256,384]{1,0:T(8,128)(2,1)}, u32[]{:S(2)}) copy-start(bf16[256,384]{1,0:T(8,128)(2,1)} %constant.4.clone.fwd) | copy-start | bytes 589828
  3.0 0.9 %copy-start.3 = (bf16[128,512]{1,0:T(8,128)(2,1)S(1)}, bf16[128,512]{1,0:T(8,128)(2,1)}, u32[]{:S(2)}) copy-start(bf16[128,512]{1,0:T(8,128)(2,1)} %w.1) | copy-start | bytes 393220
  3.9 0.8 %copy-start.4 = (f32[3,7,512]{2,1,0:T(8,128)S(1)}, f32[3,7,512]{2,1,0:T(8,128)}, u32[]{:S(2)}) copy-start(f32[3,7,512]{2,1,0:T(8,128)} %sf.1) | copy-start | bytes 129028
  4.7 0.8 %copy-start.5 = (f32[16,512]{1,0:T(8,128)S(1)}, f32[16,512]{1,0:T(8,128)}, u32[]{:S(2)}) copy-start(f32[16,512]{1,0:T(8,128)} %res.1) | copy-start | bytes 98308
  5.5 0.8 %copy-start.6 = (f32[16,512]{1,0:T(8,128)S(1)}, f32[16,512]{1,0:T(8,128)}, u32[]{:S(2)}) copy-start(f32[16,512]{1,0:T(8,128)} %dec.1) | copy-start | bytes 98308
  6.2 0.7 %copy-start.7 = (s32[16]{0:T(128)S(1)}, s32[16]{0:T(128)}, u32[]{:S(2)}) copy-start(s32[16]{0:T(128)} %docs.1) | copy-start | bytes 196

commit v2 on v1

--- a/solution.py
+++ b/solution.py
@@ -37,11 +37,11 @@
 
 
 def kernel(
-    proj, sf, res, dec, docs, w, fwd, inv, out,
-    halo, ext, query, source, spec, intra, head, hspec,
-    parts, rx, back, rx2, dparts, through, state, ends_own,
-    wbuf, hbuf, acc,
-    halo_sem, a2a_sem, ws, wr, hs, hr,
+    proj_in, sf_in, res_in, dec_in, docs_in, w, fwd_in, inv_in, out,
+    proj, sf, res, dec, docs, fwd, inv, halo, ext, query, source, spec, intra, head, hspec,
+    parts, rx, back, state, through, ends_own,
+    wbuf, hbuf, acc, outv,
+    in_sem, halo_sem, out_send, out_recv, back_send, back_recv, ws, wr, hs, hr, done,
 ):
     p, q = lax.axis_index("ctx"), lax.axis_index("ch")
     n_ctx = lax.axis_size("ctx")
@@ -67,19 +67,60 @@
             device_id=(to_ctx, to_ch), device_id_type=MESH,
         )
 
+    pairs = ((proj_in, proj), (sf_in, sf), (res_in, res), (dec_in, dec), (docs_in, docs), (fwd_in, fwd), (inv_in, inv))
+    loads = [pltpu.make_async_copy(src, dst, in_sem.at[i]) for i, (src, dst) in enumerate(pairs)]
+    hi_own = pl.ds(core * 128, 128)
+    loads.append(pltpu.make_async_copy(w, wbuf.at[y_hi, z, hi_own, :], in_sem.at[len(pairs)]))
+    for load in loads:
+        load.start()
+
+    group = p // 8
+    scans = z < 4
+    serves = 2 * y_hi + core
+    tile = z % 4
+
+    def scanner(i):
+        return (i // 8) * 16 + (i % 4) * 2 + (i // 4) % 2
+
     barrier = pltpu.get_barrier_semaphore()
 
-    def greet(o, carry):
-        pl.semaphore_signal(barrier, inc=1, device_id=((p + o) % n_ctx, q), device_id_type=MESH)
-        return carry
-
-    lax.fori_loop(1, n_ctx, greet, 0)
+    def greet(to_ctx, to_ch):
+        pl.semaphore_signal(barrier, inc=1, device_id=(to_ctx, to_ch), device_id_type=MESH)
+
+    greet((p + n_ctx - 1) % n_ctx, q)
+    toward = (z - (1 - 2 * core) + 8) % 8
+    for c in range(2):
+        greet(ctx_of(y_hi, toward, c), q)
+    greet(ctx_of(y_hi, z, 1 - core), q)
+    greet(ctx_of(1 - y_hi, z, core), q)
     for to in (q_right, q_left, q_y):
-        pl.semaphore_signal(barrier, inc=1, device_id=(p, to), device_id_type=MESH)
-    pl.semaphore_wait(barrier, n_ctx - 1 + 3)
+        greet(p, to)
+
+    def greet_scanner(i, carry):
+        @pl.when(scanner(i) != p)
+        def _():
+            greet(scanner(i), q)
+
+        return carry
+
+    lax.fori_loop(4 * group, 4 * group + 4, greet_scanner, 0)
+
+    @pl.when(scans)
+    def _():
+        def greet_member(n, carry):
+            @pl.when(n != p)
+            def _():
+                greet(n, q)
+
+            return carry
+
+        lax.fori_loop(0, 8 * serves + 8, greet_member, 0)
+
+    own_scan = jnp.where(scans, 1, 0)
+    pl.semaphore_wait(barrier, 8 + (16 - 4 * group - own_scan) + own_scan * (7 + core))
 
     halo_copy = remote(
-        proj.at[:, pl.ds(240, 16), :], halo, halo_sem.at[0], halo_sem.at[1], (p + 1) % n_ctx, q
+        proj_in.at[:, pl.ds(240, 16), :], halo, halo_sem.at[0], halo_sem.at[1], (p + 1) % n_ctx, q
     )
     halo_copy.start()
 
@@ -128,7 +169,8 @@
     started(
         remote(w, half(y_hi, z, core), ws.at[1, 0], wr.at[1, 0], ctx_of(1 - y_hi, z, core), q)
     )
-    half(y_hi, z, core)[...] = w[...]
+    for load in loads:
+        load.wait()
 
     begins0, begins1, at = jnp.float32(0), jnp.float32(0), jnp.int32(0)
     rows = lax.broadcasted_iota(jnp.int32, (32, LANES), 0)
@@ -146,27 +188,27 @@
     def lane(t):
         return pl.ds(pl.multiple_of(t * LANES, LANES), LANES)
 
+    def wide(a):
+        return jnp.broadcast_to(a[:, None, :], (ORDER, 8, LANES))
+
     def head_tile(t, carry):
         d = dec[:, lane(t)]
-        lam8 = jnp.exp(-8.0 * d)[:, None, :]
-        v = res[:, lane(t)][:, None, :] * jnp.exp(-d[:, None, :] * sub)
+        lam8 = wide(jnp.exp(-8.0 * d))
+        v = wide(res[:, lane(t)]) * jnp.exp(-d[:, None, :] * sub)
         pieces = []
         for k in range(BLK // 8):
             pieces.append(jnp.sum(v, axis=0))
             v = v * lam8
         head[:, lane(t)] = jnp.concatenate(pieces, axis=0)
-        for i in range(8):
-            dparts[i * tiles + t] = d[2 * i : 2 * i + 2]
         return carry
 
     lax.fori_loop(0, tiles, head_tile, 0)
     hspec[...] = jnp.dot(fwd[...], split_rows(head[...]), preferred_element_type=F32) * (1.0 / BLK)
-    lam256 = jnp.exp(-256.0 * dparts[p])
+    lam256 = jnp.exp(-256.0 * dec[:, lane(tile)])
     for n in range(32):
         through[n] = lam256 * unbroken[n : n + 1, :]
 
-    halo_copy.wait()
-    for s in range(3):
+    def extend(s):
         for j in range(2):
             if j == 0:
                 before = halo[s, :, :].astype(F32)[8:16]
@@ -177,67 +219,105 @@
             ext[s, j, 0:8, :] = before
             ext[s, j, 8:136, :] = proj[s, j * BLK : (j + 1) * BLK, :].astype(F32)
 
-    def short_tile(t, carry):
+    def short(s, j, t):
+        total = jnp.zeros((BLK, LANES), F32)
+        for tap in range(SHORT):
+            total = total + sf[s, tap : tap + 1, lane(t)] * ext[s, j, 8 - tap : 136 - tap, lane(t)]
+        return total
+
+    def both_lanes(j, t):
+        return pl.ds(pl.multiple_of(j * tiles * LANES + t * LANES, LANES), LANES)
+
+    def source_tile(t, carry):
         for j in range(2):
-            short = []
-            for s in range(3):
-                total = jnp.zeros((BLK, LANES), F32)
-                for tap in range(SHORT):
-                    total = total + sf[s, tap : tap + 1, lane(t)] * ext[s, j, 8 - tap : 136 - tap, lane(t)]
-                short.append(total)
-            query[j, :, lane(t)] = short[0]
-            source[:, pl.ds(pl.multiple_of(j * tiles * LANES + t * LANES, LANES), LANES)] = short[1] * short[2]
-        return carry
-
-    lax.fori_loop(0, tiles, short_tile, 0)
+            source[:, both_lanes(j, t)] = short(1, j, t) * short(2, j, t)
+        return carry
+
+    def query_tile(t, carry):
+        for j in range(2):
+            query[j, :, lane(t)] = short(0, j, t)
+        return carry
+
+    halo_copy.wait()
+    extend(1)
+    extend(2)
+    lax.fori_loop(0, tiles, source_tile, 0)
 
     def end_tile(t, carry):
         d = dec[:, lane(t)]
-        lam8 = jnp.exp(-8.0 * d)[:, None, :]
+        lam8 = wide(jnp.exp(-8.0 * d))
         lam128 = jnp.exp(-128.0 * d)
         weight = jnp.exp(-d[:, None, :] * (7.0 - sub))
         own = []
         for j in range(2):
-            lanes = pl.ds(pl.multiple_of(j * tiles * LANES + t * LANES, LANES), LANES)
+            lanes = both_lanes(j, t)
             total = jnp.zeros((ORDER, 8, LANES), F32)
             for k in range(BLK // 8):
                 total = total * lam8 + source[8 * k : 8 * k + 8, lanes][None]
             own.append(jnp.sum(total * weight, axis=1))
         ends_own[:, lane(t)] = own[0]
         final = own[1] + lam128 * own[0] * goes1
-        for i in range(8):
-            parts[i * tiles + t] = final[2 * i : 2 * i + 2]
+        parts[t] = final
         return carry
 
     lax.fori_loop(0, tiles, end_tile, 0)
 
-    def to_all(src, dst, send, recv):
-        def one(o, carry):
-            to = (p + o) % n_ctx
-            remote(src.at[to], dst.at[p], send, recv, to, q).start()
-            return carry
-
-        lax.fori_loop(1, n_ctx, one, 0)
-        dst[p] = src[p]
-
-    def all_in(buf, sem):
-        landed(buf.at[pl.ds(0, 31)], sem)
-
-    to_all(parts, rx, a2a_sem.at[0], a2a_sem.at[1])
-    pass_on(0, 1)
+    def hand_out(i, carry):
+        @pl.when(scanner(i) != p)
+        def _():
+            remote(parts.at[i % 4], rx.at[p], out_send.at[i], out_recv.at[group], scanner(i), q).start()
+
+        return carry
+
+    lax.fori_loop(4 * group, 16, hand_out, 0)
+
     seed = half(1 - y_hi, z, core)
     landed(seed, wr.at[1, 0])
     spread(1, seed)
+    pass_on(0, 1)
+    extend(0)
+    lax.fori_loop(0, tiles, query_tile, 0)
     spec[...] = jnp.dot(fwd[...], split_rows(source[...]), preferred_element_type=F32)
-    all_in(rx, a2a_sem.at[1])
-
-    def scan(n, s):
-        back[n] = s
-        return s * through[n] + rx[n]
-
-    lax.fori_loop(0, 32, scan, jnp.zeros((2, LANES), F32))
-    to_all(back, rx2, a2a_sem.at[2], a2a_sem.at[3])
-    pass_on(0, 2)
+
+    @pl.when(scans)
+    def _():
+        rx[p] = parts[tile]
+
+        def earlier(g, s):
+            landed(rx.at[pl.ds(0, 8)], out_recv.at[g])
+            for n in range(8):
+                s = s * through[8 * g + n] + rx[8 * g + n]
+            return s
+
+        s = lax.fori_loop(0, group, earlier, jnp.zeros((ORDER, LANES), F32))
+        landed(rx.at[pl.ds(0, 7)], out_recv.at[group])
+
+        def own_group(g, s):
+            for n in range(8):
+                s = s * through[8 * g + n] + rx[8 * g + n]
+            return s
+
+        s = lax.fori_loop(group, group + core, own_group, s)
+
+        @pl.when(core == 1)
+        def _():
+            landed(rx.at[pl.ds(0, 8)], out_recv.at[serves])
+
+        for n in range(8):
+            back[n] = s
+            if n < 7:
+                s = s * through[8 * serves + n] + rx[8 * serves + n]
+        for n in range(8):
+
+            @pl.when(8 * serves + n != p)
+            def _():
+                remote(back.at[n], state.at[tile], back_send.at[n], back_recv.at[0], 8 * serves + n, q).start()
+
+        @pl.when(core == 0)
+        def _():
+            state[tile] = back[p % 8]
+
+    pass_on(1, 1)
 
     chans = proj.shape[2]
     for j in range(2):
@@ -248,21 +328,26 @@
         y_im = s_re * h_im + s_im * h_re
         both = jnp.concatenate([y_re, y_im], axis=0)
         intra[j] = jnp.dot(inv[...], split_rows(both), preferred_element_type=F32)
-    pass_on(1, 1)
-
-    all_in(rx2, a2a_sem.at[3])
-    for t in range(tiles):
-        for i in range(8):
-            state[2 * i : 2 * i + 2, t * LANES : (t + 1) * LANES] = rx2[i * tiles + t]
+    pass_on(0, 2)
+
+    own_part = jnp.logical_and(scans, core == 0)
+
+    @pl.when(own_part)
+    def _():
+        landed(state.at[pl.ds(0, 3)], back_recv.at[0])
+
+    @pl.when(jnp.logical_not(own_part))
+    def _():
+        landed(state, back_recv.at[0])
 
     def hidden_block(j):
         def hidden_tile(t, carry):
             d = dec[:, lane(t)]
-            lam8 = jnp.exp(-8.0 * d)[:, None, :]
-            entering = state[:, lane(t)] * goes0
+            lam8 = wide(jnp.exp(-8.0 * d))
+            entering = state[t] * goes0
             if j == 1:
                 entering = (jnp.exp(-128.0 * d) * entering + ends_own[:, lane(t)]) * goes1
-            v = (res[:, lane(t)] * entering)[:, None, :] * jnp.exp(-d[:, None, :] * (sub + 1.0))
+            v = wide(res[:, lane(t)] * entering) * jnp.exp(-d[:, None, :] * (sub + 1.0))
             pieces = []
             for k in range(BLK // 8):
                 pieces.append(jnp.sum(v, axis=0))
@@ -287,20 +372,20 @@
         give(0 + j, q, j, q_right)
         give(2 + j, q, j, q_left)
         give(4 + j, q, j, q_y)
-    pass_on(0, 3)
     pass_on(1, 2)
     took(0, q_left, 0)
     give(6, q_left, 0, q_right)
     give(8, q_left, 0, q_y)
     took(2, q_right, 0)
     give(9, q_right, 0, q_y)
+    pass_on(0, 3)
     took(3, q_right, 1)
     give(7, q_right, 1, q_left)
     took(5, q_y, 1)
     give(10, q_y, 1, q_right)
     give(11, q_y, 1, q_left)
+    pass_on(1, 3)
     pass_on(0, 4)
-    pass_on(1, 3)
     took(8, q_yleft, 0)
     give(12, q_yleft, 0, q_right)
     took(11, q_yright, 1)
@@ -313,44 +398,72 @@
         for hop in range(1, 5):
             oz = (z + step * hop + 8) % 8
             landed(wbuf.at[hi, oz] if hop < 4 else half(hi, oz, 1 - core), wr.at[plane, 6 + hop])
-    took(1, q_left, 1)
-    took(4, q_y, 0)
-    took(6, q_opp, 0)
-    took(7, q_opp, 1)
-    took(9, q_yright, 0)
-    took(10, q_yleft, 1)
-
-    acc[...] = jnp.zeros_like(acc)
+
+    def product(b):
+        weights = wbuf[b // 4, pl.ds(2 * (b % 4), 2)].reshape(4 * BLK, acc.shape[1])
+        return jnp.dot(hbuf[b], weights, preferred_element_type=F32)
 
     def project(k, carry):
         m = k % 4
         dx = m + (m // 2) * (1 - 2 * (m % 2))
-        b = ((y_lo + k // 4) % 2) * 4 + (x + dx) % 4
-        weights = wbuf[b // 4, pl.ds(2 * (b % 4), 2)].reshape(4 * BLK, acc.shape[1])
-        acc[...] += jnp.dot(hbuf[b], weights, preferred_element_type=F32)
-        return carry
-
-    lax.fori_loop(0, 7, project, 0)
+        acc[...] += product(((y_lo + k // 4) % 2) * 4 + (x + dx) % 4)
+        return carry
+
+    took(1, q_left, 1)
+    took(4, q_y, 0)
+    acc[...] = product(q_y)
+    lax.fori_loop(0, 3, project, 0)
+    took(6, q_opp, 0)
+    took(7, q_opp, 1)
+    lax.fori_loop(3, 4, project, 0)
+    took(9, q_yright, 0)
+    took(10, q_yleft, 1)
+    lax.fori_loop(5, 7, project, 0)
     took(12, q_yopp, 0)
     took(13, q_yopp, 1)
-    lax.fori_loop(7, 8, project, 0)
-    out[...] = acc[...].astype(BF16)
+    outv[...] = (acc[...] + product(q_yopp)).astype(BF16)
+    result = pltpu.make_async_copy(outv, out, done.at[0])
+    result.start()
 
     for copy in sends:
         copy.wait_send()
-    landed(parts.at[pl.ds(0, 31)], a2a_sem.at[0])
-    landed(back.at[pl.ds(0, 31)], a2a_sem.at[2])
+
+    def handed_out(i, carry):
+        @pl.when(scanner(i) != p)
+        def _():
+            landed(parts.at[i % 4], out_send.at[i])
+
+        return carry
+
+    lax.fori_loop(4 * group, 16, handed_out, 0)
+
+    @pl.when(scans)
+    def _():
+        for n in range(8):
+
+            @pl.when(8 * serves + n != p)
+            def _():
+                landed(back.at[n], back_send.at[n])
+
+    result.wait()
 
 
 def shards(fwd, inv, projected, short_filter, residues, decay_rates, doc_blocks, out_weight):
     rows, chans = projected.shape[1:]
-    vmem = pl.BlockSpec(memory_space=pltpu.VMEM)
+    hbm = pl.BlockSpec(memory_space=pltpu.HBM)
     return pl.pallas_call(
         kernel,
         out_shape=jax.ShapeDtypeStruct((rows, out_weight.shape[1]), BF16),
-        in_specs=[vmem] * 4 + [pl.BlockSpec(memory_space=pltpu.SMEM)] + [vmem] * 3,
-        out_specs=vmem,
+        in_specs=[hbm] * 8,
+        out_specs=hbm,
         scratch_shapes=[
+            pltpu.VMEM(projected.shape, BF16),
+            pltpu.VMEM(short_filter.shape, F32),
+            pltpu.VMEM(residues.shape, F32),
+            pltpu.VMEM(decay_rates.shape, F32),
+            pltpu.SMEM(doc_blocks.shape, jnp.int32),
+            pltpu.VMEM(fwd.shape, BF16),
+            pltpu.VMEM(inv.shape, BF16),
             pltpu.VMEM((3, 16, chans), BF16),
             pltpu.VMEM((3, 2, 8 + BLK, chans), F32),
             pltpu.VMEM((2, BLK, chans), F32),
@@ -359,26 +472,30 @@
             pltpu.VMEM((2, BLK, chans), F32),
             pltpu.VMEM((BLK, chans), F32),
             pltpu.VMEM((2 * BLK, chans), F32),
-            pltpu.VMEM((32, 2, LANES), F32),
-            pltpu.VMEM((32, 2, LANES), F32),
-            pltpu.VMEM((32, 2, LANES), F32),
-            pltpu.VMEM((32, 2, LANES), F32),
-            pltpu.VMEM((32, 2, LANES), F32),
-            pltpu.VMEM((32, 2, LANES), F32),
-            pltpu.VMEM((ORDER, chans), F32),
+            pltpu.VMEM((4, ORDER, LANES), F32),
+            pltpu.VMEM((32, ORDER, LANES), F32),
+            pltpu.VMEM((8, ORDER, LANES), F32),
+            pltpu.VMEM((4, ORDER, LANES), F32),
+            pltpu.VMEM((32, ORDER, LANES), F32),
             pltpu.VMEM((ORDER, chans), F32),
             pltpu.VMEM((2, 8, 2 * BLK, out_weight.shape[1]), BF16),
             pltpu.VMEM((8, rows, chans), BF16),
             pltpu.VMEM((rows, out_weight.shape[1]), F32),
+            pltpu.VMEM((rows, out_weight.shape[1]), BF16),
+            pltpu.SemaphoreType.DMA((8,)),
             pltpu.SemaphoreType.DMA((2,)),
+            pltpu.SemaphoreType.DMA((16,)),
             pltpu.SemaphoreType.DMA((4,)),
+            pltpu.SemaphoreType.DMA((8,)),
+            pltpu.SemaphoreType.DMA((1,)),
             pltpu.SemaphoreType.DMA((2, 11)),
             pltpu.SemaphoreType.DMA((2, 11)),
             pltpu.SemaphoreType.DMA((14,)),
             pltpu.SemaphoreType.DMA((14,)),
+            pltpu.SemaphoreType.DMA((1,)),
         ],
         compiler_params=pltpu.CompilerParams(
-            collective_id=0, has_side_effects=True, vmem_limit_bytes=40 * 1024 * 1024
+            collective_id=0, has_side_effects=True, vmem_limit_bytes=60 * 1024 * 1024
         ),
         name="hyena_block",
     )(projected, short_filter, residues, decay_rates, doc_blocks, out_weight, fwd, inv)

time: 57.5 us -> 48.1 us (0.84)
  local copies, waits for them, and re-layouts: 7.56 us -> 1.67 us
  Pallas kernels: 49.6 us -> 45.7 us
    unnamed x17 -> x1, local copies, waits for them, and re-layouts: 7.56 us -> 1.67 us
    pallas_call x1, Pallas kernels: 49.6 us -> 45.7 us  [shards(): pl.pallas_call(kernel, out_shape=jax.ShapeDtypeStruct((rows, out_weight.s...]
where the time goes in v2:
time: 48.1 us; the launch traced here: 47.3 us
  Pallas kernels  45.7 us (95%)
  local copies, waits for them, and re-layouts  1.67 us (3%)
    pallas_call x1, Pallas kernels, shards(): pl.pallas_call(kernel, out_shape=jax.ShapeDtypeStruct((rows, out_weight.s...  45.7 us
    unnamed x1, local copies, waits for them, and re-layouts  1.67 us

profile of v2, /device:TPU:1, one launch (start us, length us, event | category | flops | bytes accessed | tf_op | source)
XLA Modules:
  0.0 47.3 jit_solution(12190104973823389498)
XLA Ops:
  0.0 45.7 %hyena_block.1 = bf16[256,512]{1,0:T(8,128)(2,1)} custom-call(bf16[3,256,512]{2,1,0:T(8,128)(2,1)} %proj_in.1, f32[3,7,512]{2,1,0:T(8,128)} %sf_in.1, f32[16,512]{1,0:T(8,128)} %res_in.1, f32[16,512]{1,0:T(8,128)} %dec_in.1, s32[16]{0:T(128)} %docs_in.1, bf16[128,512]{1,0:T(8,128)(2,1)} %w.1, bf16[256,384]{1,0:T(8,128)(2,1)} %constant.4.clone.fwd_in, ...), custom_call_target="tpu_custom_call" | custom-call | tf_op jit(solution)/shard_map/hyena_block/pallas_call | solution.py:454
  45.7 1.7 %copy.10 = bf16[256,512]{1,0:T(8,128)(2,1)} copy(bf16[256,512]{1,0:T(8,128)(2,1)} %hyena_block.1) | data formatting | bytes 524288

commit v3 on v2

--- a/solution.py
+++ b/solution.py
@@ -39,9 +39,9 @@
 def kernel(
     proj_in, sf_in, res_in, dec_in, docs_in, w, fwd_in, inv_in, out,
     proj, sf, res, dec, docs, fwd, inv, halo, ext, query, source, spec, intra, head, hspec,
-    parts, rx, back, state, through, ends_own,
-    wbuf, hbuf, acc, outv,
-    in_sem, halo_sem, out_send, out_recv, back_send, back_recv, ws, wr, hs, hr, done,
+    parts, rx, back, state, through, ends_own, ends_next, lam8, lam128, first_weight, reach,
+    wbuf, hbuf, acc,
+    in_sem, halo_sem, out_send, out_recv, back_send, back_recv, ws, wr, hs, hr,
 ):
     p, q = lax.axis_index("ctx"), lax.axis_index("ch")
     n_ctx = lax.axis_size("ctx")
@@ -191,92 +191,104 @@
     def wide(a):
         return jnp.broadcast_to(a[:, None, :], (ORDER, 8, LANES))
 
-    def head_tile(t, carry):
-        d = dec[:, lane(t)]
-        lam8 = wide(jnp.exp(-8.0 * d))
-        v = wide(res[:, lane(t)]) * jnp.exp(-d[:, None, :] * sub)
-        pieces = []
-        for k in range(BLK // 8):
-            pieces.append(jnp.sum(v, axis=0))
-            v = v * lam8
-        head[:, lane(t)] = jnp.concatenate(pieces, axis=0)
-        return carry
-
-    lax.fori_loop(0, tiles, head_tile, 0)
-    hspec[...] = jnp.dot(fwd[...], split_rows(head[...]), preferred_element_type=F32) * (1.0 / BLK)
-    lam256 = jnp.exp(-256.0 * dec[:, lane(tile)])
-    for n in range(32):
-        through[n] = lam256 * unbroken[n : n + 1, :]
+    def wide(a):
+        return jnp.broadcast_to(a[:, None, :], (ORDER, 8, LANES))
 
     def extend(s):
         for j in range(2):
-            if j == 0:
-                before = halo[s, :, :].astype(F32)[8:16]
-                before = jnp.where(goes0 > 0.5, before, 0.0)
-            else:
+            if j == 1:
                 before = proj[s, 112:128, :].astype(F32)[8:16]
-                before = jnp.where(goes1 > 0.5, before, 0.0)
-            ext[s, j, 0:8, :] = before
+                ext[s, j, 0:8, :] = jnp.where(goes1 > 0.5, before, 0.0)
             ext[s, j, 8:136, :] = proj[s, j * BLK : (j + 1) * BLK, :].astype(F32)
 
-    def short(s, j, t):
-        total = jnp.zeros((BLK, LANES), F32)
+    def extend_from_halo(s):
+        before = halo[s, :, :].astype(F32)[8:16]
+        ext[s, 0, 0:8, :] = jnp.where(goes0 > 0.5, before, 0.0)
+
+    def short(s, j, t, begin, end):
+        total = jnp.zeros((end - begin, LANES), F32)
         for tap in range(SHORT):
-            total = total + sf[s, tap : tap + 1, lane(t)] * ext[s, j, 8 - tap : 136 - tap, lane(t)]
+            total = total + sf[s, tap : tap + 1, lane(t)] * ext[s, j, begin + 8 - tap : end + 8 - tap, lane(t)]
         return total
 
     def both_lanes(j, t):
         return pl.ds(pl.multiple_of(j * tiles * LANES + t * LANES, LANES), LANES)
 
-    def source_tile(t, carry):
+    def local_tile(t, carry):
+        source[8:BLK, both_lanes(0, t)] = short(1, 0, t, 8, BLK) * short(2, 0, t, 8, BLK)
+        source[:, both_lanes(1, t)] = short(1, 1, t, 0, BLK) * short(2, 1, t, 0, BLK)
+        d = dec[:, lane(t)]
+        step8 = wide(jnp.exp(-8.0 * d))
+        lam8[t] = step8
+        weight = jnp.exp(-d[:, None, :] * (7.0 - sub))
         for j in range(2):
-            source[:, both_lanes(j, t)] = short(1, j, t) * short(2, j, t)
+            total = jnp.zeros((ORDER, 8, LANES), F32)
+            for k in range(1 - j, BLK // 8):
+                total = total * step8 + source[8 * k : 8 * k + 8, both_lanes(j, t)][None]
+            own = jnp.sum(total * weight, axis=1)
+            if j == 0:
+                ends_own[:, lane(t)] = own
+            else:
+                ends_next[:, lane(t)] = own
+        first_weight[t] = jnp.exp(-d[:, None, :] * (127.0 - sub))
+        lam128[:, lane(t)] = jnp.exp(-128.0 * d)
+        return carry
+
+    def halo_tile(t, carry):
+        first = short(1, 0, t, 0, 8) * short(2, 0, t, 0, 8)
+        source[0:8, both_lanes(0, t)] = first
+        own = ends_own[:, lane(t)] + jnp.sum(first_weight[t] * first[None], axis=1)
+        ends_own[:, lane(t)] = own
+        parts[t] = ends_next[:, lane(t)] + lam128[:, lane(t)] * own * goes1
         return carry
 
     def query_tile(t, carry):
         for j in range(2):
-            query[j, :, lane(t)] = short(0, j, t)
-        return carry
-
-    halo_copy.wait()
+            query[j, :, lane(t)] = short(0, j, t, 0, BLK)
+        return carry
+
     extend(1)
     extend(2)
-    lax.fori_loop(0, tiles, source_tile, 0)
-
-    def end_tile(t, carry):
-        d = dec[:, lane(t)]
-        lam8 = wide(jnp.exp(-8.0 * d))
-        lam128 = jnp.exp(-128.0 * d)
-        weight = jnp.exp(-d[:, None, :] * (7.0 - sub))
-        own = []
-        for j in range(2):
-            lanes = both_lanes(j, t)
-            total = jnp.zeros((ORDER, 8, LANES), F32)
-            for k in range(BLK // 8):
-                total = total * lam8 + source[8 * k : 8 * k + 8, lanes][None]
-            own.append(jnp.sum(total * weight, axis=1))
-        ends_own[:, lane(t)] = own[0]
-        final = own[1] + lam128 * own[0] * goes1
-        parts[t] = final
-        return carry
-
-    lax.fori_loop(0, tiles, end_tile, 0)
-
-    def hand_out(i, carry):
-        @pl.when(scanner(i) != p)
+    lax.fori_loop(0, tiles, local_tile, 0)
+
+    @pl.when(scans)
+    def _():
+        lam256 = jnp.exp(-256.0 * dec[:, lane(tile)])
+        for n in range(32):
+            through[n] = lam256 * unbroken[n : n + 1, :]
+
+    halo_copy.wait()
+    extend_from_halo(1)
+    extend_from_halo(2)
+    lax.fori_loop(0, tiles, halo_tile, 0)
+
+    for i in range(16):
+
+        @pl.when(jnp.logical_and(i >= 4 * group, p != scanner(i)))
         def _():
             remote(parts.at[i % 4], rx.at[p], out_send.at[i], out_recv.at[group], scanner(i), q).start()
-
-        return carry
-
-    lax.fori_loop(4 * group, 16, hand_out, 0)
 
     seed = half(1 - y_hi, z, core)
     landed(seed, wr.at[1, 0])
     spread(1, seed)
     pass_on(0, 1)
     extend(0)
+    extend_from_halo(0)
     lax.fori_loop(0, tiles, query_tile, 0)
+    def head_tile(t, carry):
+        d = dec[:, lane(t)]
+        step8 = lam8[t]
+        v = wide(res[:, lane(t)]) * jnp.exp(-d[:, None, :] * sub)
+        reach[t] = wide(res[:, lane(t)]) * jnp.exp(-d[:, None, :] * (sub + 1.0))
+        pieces = []
+        for k in range(BLK // 8):
+            pieces.append(jnp.sum(v, axis=0))
+            v = v * step8
+        head[:, lane(t)] = jnp.concatenate(pieces, axis=0)
+        return carry
+
+    lax.fori_loop(0, tiles, head_tile, 0)
+    hspec[...] = jnp.dot(fwd[...], split_rows(head[...]), preferred_element_type=F32) * (1.0 / BLK)
     spec[...] = jnp.dot(fwd[...], split_rows(source[...]), preferred_element_type=F32)
 
     @pl.when(scans)
@@ -342,16 +354,15 @@
 
     def hidden_block(j):
         def hidden_tile(t, carry):
-            d = dec[:, lane(t)]
-            lam8 = wide(jnp.exp(-8.0 * d))
+            step8 = lam8[t]
             entering = state[t] * goes0
             if j == 1:
-                entering = (jnp.exp(-128.0 * d) * entering + ends_own[:, lane(t)]) * goes1
-            v = wide(res[:, lane(t)] * entering) * jnp.exp(-d[:, None, :] * (sub + 1.0))
+                entering = (lam128[:, lane(t)] * entering + ends_own[:, lane(t)]) * goes1
+            v = wide(entering) * reach[t]
             pieces = []
             for k in range(BLK // 8):
                 pieces.append(jnp.sum(v, axis=0))
-                v = v * lam8
+                v = v * step8
             response = intra[j, :, lane(t)] + jnp.concatenate(pieces, axis=0)
             hbuf[q, j * BLK : (j + 1) * BLK, lane(t)] = (query[j, :, lane(t)] * response).astype(BF16)
             return carry
@@ -367,29 +378,32 @@
     def took(idx, b, j):
         landed(piece(b, j), hr.at[idx])
 
-    for j in range(2):
-        hidden_block(j)
-        give(0 + j, q, j, q_right)
-        give(2 + j, q, j, q_left)
-        give(4 + j, q, j, q_y)
+    hidden_block(0)
+    give(0, q, 0, q_right)
+    hidden_block(1)
+    give(3, q, 1, q_left)
+    give(5, q, 1, q_y)
+    give(1, q, 1, q_right)
+    give(2, q, 0, q_left)
+    give(4, q, 0, q_y)
     pass_on(1, 2)
     took(0, q_left, 0)
     give(6, q_left, 0, q_right)
     give(8, q_left, 0, q_y)
+    took(5, q_y, 1)
+    give(11, q_y, 1, q_left)
+    give(10, q_y, 1, q_right)
+    took(3, q_right, 1)
+    give(7, q_right, 1, q_left)
+    pass_on(0, 3)
     took(2, q_right, 0)
     give(9, q_right, 0, q_y)
-    pass_on(0, 3)
-    took(3, q_right, 1)
-    give(7, q_right, 1, q_left)
-    took(5, q_y, 1)
-    give(10, q_y, 1, q_right)
-    give(11, q_y, 1, q_left)
     pass_on(1, 3)
-    pass_on(0, 4)
     took(8, q_yleft, 0)
     give(12, q_yleft, 0, q_right)
     took(11, q_yright, 1)
     give(13, q_yright, 1, q_left)
+    pass_on(0, 4)
     pass_on(1, 4)
 
     for plane in range(2):
@@ -421,9 +435,7 @@
     lax.fori_loop(5, 7, project, 0)
     took(12, q_yopp, 0)
     took(13, q_yopp, 1)
-    outv[...] = (acc[...] + product(q_yopp)).astype(BF16)
-    result = pltpu.make_async_copy(outv, out, done.at[0])
-    result.start()
+    out[...] = (acc[...] + product(q_yopp)).astype(BF16)
 
     for copy in sends:
         copy.wait_send()
@@ -444,8 +456,6 @@
             @pl.when(8 * serves + n != p)
             def _():
                 landed(back.at[n], back_send.at[n])
-
-    result.wait()
 
 
 def shards(fwd, inv, projected, short_filter, residues, decay_rates, doc_blocks, out_weight):
@@ -453,9 +463,9 @@
     hbm = pl.BlockSpec(memory_space=pltpu.HBM)
     return pl.pallas_call(
         kernel,
-        out_shape=jax.ShapeDtypeStruct((rows, out_weight.shape[1]), BF16),
+        out_shape=pltpu.VMEM((rows, out_weight.shape[1]), BF16),
         in_specs=[hbm] * 8,
-        out_specs=hbm,
+        out_specs=pl.BlockSpec(memory_space=pltpu.VMEM),
         scratch_shapes=[
             pltpu.VMEM(projected.shape, BF16),
             pltpu.VMEM(short_filter.shape, F32),
@@ -478,10 +488,14 @@
             pltpu.VMEM((4, ORDER, LANES), F32),
             pltpu.VMEM((32, ORDER, LANES), F32),
             pltpu.VMEM((ORDER, chans), F32),
+            pltpu.VMEM((ORDER, chans), F32),
+            pltpu.VMEM((4, ORDER, 8, LANES), F32),
+            pltpu.VMEM((ORDER, chans), F32),
+            pltpu.VMEM((4, ORDER, 8, LANES), F32),
+            pltpu.VMEM((4, ORDER, 8, LANES), F32),
             pltpu.VMEM((2, 8, 2 * BLK, out_weight.shape[1]), BF16),
             pltpu.VMEM((8, rows, chans), BF16),
             pltpu.VMEM((rows, out_weight.shape[1]), F32),
-            pltpu.VMEM((rows, out_weight.shape[1]), BF16),
             pltpu.SemaphoreType.DMA((8,)),
             pltpu.SemaphoreType.DMA((2,)),
             pltpu.SemaphoreType.DMA((16,)),
@@ -492,7 +506,6 @@
             pltpu.SemaphoreType.DMA((2, 11)),
             pltpu.SemaphoreType.DMA((14,)),
             pltpu.SemaphoreType.DMA((14,)),
-            pltpu.SemaphoreType.DMA((1,)),
         ],
         compiler_params=pltpu.CompilerParams(
             collective_id=0, has_side_effects=True, vmem_limit_bytes=60 * 1024 * 1024

time: 48.1 us -> 45.7 us (0.950); the launches traced: 47.3 us -> 45.6 us
  local copies, waits for them, and re-layouts: 1.67 us -> 0.71 us
  Pallas kernels: 45.7 us -> 44.9 us
    unnamed x1, local copies, waits for them, and re-layouts: 1.67 us -> 0.71 us
    pallas_call x1, Pallas kernels: 45.7 us -> 44.9 us  [shards(): pl.pallas_call(kernel, out_shape=pltpu.VMEM((rows, out_weight.shape[1]),...]
where the time goes in v3:
time: 45.7 us; the launch traced here: 45.6 us
  Pallas kernels  44.9 us (98%)
  local copies, waits for them, and re-layouts  0.71 us (2%)
    pallas_call x1, Pallas kernels, shards(): pl.pallas_call(kernel, out_shape=pltpu.VMEM((rows, out_weight.shape[1]),...  44.9 us

profile of v3, /device:TPU:1, one launch (start us, length us, event | category | flops | bytes accessed | tf_op | source)
XLA Modules:
  0.0 45.6 jit_solution(7355154663664619178)
XLA Ops:
  0.0 44.9 %hyena_block.1 = bf16[256,512]{1,0:T(8,128)(2,1)S(1)} custom-call(bf16[3,256,512]{2,1,0:T(8,128)(2,1)} %proj_in.1, f32[3,7,512]{2,1,0:T(8,128)} %sf_in.1, f32[16,512]{1,0:T(8,128)} %res_in.1, f32[16,512]{1,0:T(8,128)} %dec_in.1, s32[16]{0:T(128)} %docs_in.1, bf16[128,512]{1,0:T(8,128)(2,1)} %w.1, bf16[256,384]{1,0:T(8,128)(2,1)} %constant.4.clone.fwd_in, ...), custom_call_target="tpu_custom_call" | custom-call | tf_op jit(solution)/shard_map/hyena_block/pallas_call | solution.py:464
  44.9 0.7 %copy.10 = bf16[256,512]{1,0:T(8,128)(2,1)} copy(bf16[256,512]{1,0:T(8,128)(2,1)S(1)} %hyena_block.1) | data formatting | bytes 524288

commit v4 on v3

--- a/solution.py
+++ b/solution.py
@@ -329,8 +329,6 @@
         def _():
             state[tile] = back[p % 8]
 
-    pass_on(1, 1)
-
     chans = proj.shape[2]
     for j in range(2):
         cols = slice(j * chans, (j + 1) * chans)
@@ -340,7 +338,7 @@
         y_im = s_re * h_im + s_im * h_re
         both = jnp.concatenate([y_re, y_im], axis=0)
         intra[j] = jnp.dot(inv[...], split_rows(both), preferred_element_type=F32)
-    pass_on(0, 2)
+    pass_on(1, 1)
 
     own_part = jnp.logical_and(scans, core == 0)
 
@@ -386,6 +384,7 @@
     give(1, q, 1, q_right)
     give(2, q, 0, q_left)
     give(4, q, 0, q_y)
+    pass_on(0, 2)
     pass_on(1, 2)
     took(0, q_left, 0)
     give(6, q_left, 0, q_right)
@@ -417,22 +416,24 @@
         weights = wbuf[b // 4, pl.ds(2 * (b % 4), 2)].reshape(4 * BLK, acc.shape[1])
         return jnp.dot(hbuf[b], weights, preferred_element_type=F32)
 
-    def project(k, carry):
-        m = k % 4
-        dx = m + (m // 2) * (1 - 2 * (m % 2))
-        acc[...] += product(((y_lo + k // 4) % 2) * 4 + (x + dx) % 4)
-        return carry
+    def project_all(blocks, first):
+        for n in range(2):
+            cols = slice(n * 256, (n + 1) * 256)
+            total = None if first else acc[:, cols]
+            for b in blocks:
+                weights = wbuf[b // 4, pl.ds(2 * (b % 4), 2), :, cols].reshape(4 * BLK, 256)
+                part = jnp.dot(hbuf[b], weights, preferred_element_type=F32)
+                total = part if total is None else total + part
+            acc[:, cols] = total
 
     took(1, q_left, 1)
     took(4, q_y, 0)
-    acc[...] = product(q_y)
-    lax.fori_loop(0, 3, project, 0)
+    project_all((q_y, q, q_right, q_left), True)
     took(6, q_opp, 0)
     took(7, q_opp, 1)
-    lax.fori_loop(3, 4, project, 0)
     took(9, q_yright, 0)
     took(10, q_yleft, 1)
-    lax.fori_loop(5, 7, project, 0)
+    project_all((q_opp, q_yright, q_yleft), False)
     took(12, q_yopp, 0)
     took(13, q_yopp, 1)
     out[...] = (acc[...] + product(q_yopp)).astype(BF16)

time: 45.7 us -> 44.5 us (0.974)
  Pallas kernels: 44.9 us -> 43.7 us
    pallas_call x1, Pallas kernels: 44.9 us -> 43.7 us  [shards(): pl.pallas_call(kernel, out_shape=pltpu.VMEM((rows, out_weight.shape[1]),...]
where the time goes in v4:
time: 44.5 us; the launch traced here: 44.4 us
  Pallas kernels  43.7 us (98%)
  local copies, waits for them, and re-layouts  0.71 us (2%)
    pallas_call x1, Pallas kernels, shards(): pl.pallas_call(kernel, out_shape=pltpu.VMEM((rows, out_weight.shape[1]),...  43.7 us

profile of v4, /device:TPU:1, one launch (start us, length us, event | category | flops | bytes accessed | tf_op | source)
XLA Modules:
  0.0 44.4 jit_solution(13992759665406682088)
XLA Ops:
  0.0 43.7 %hyena_block.1 = bf16[256,512]{1,0:T(8,128)(2,1)S(1)} custom-call(bf16[3,256,512]{2,1,0:T(8,128)(2,1)} %proj_in.1, f32[3,7,512]{2,1,0:T(8,128)} %sf_in.1, f32[16,512]{1,0:T(8,128)} %res_in.1, f32[16,512]{1,0:T(8,128)} %dec_in.1, s32[16]{0:T(128)} %docs_in.1, bf16[128,512]{1,0:T(8,128)(2,1)} %w.1, bf16[256,384]{1,0:T(8,128)(2,1)} %constant.4.clone.fwd_in, ...), custom_call_target="tpu_custom_call" | custom-call | tf_op jit(solution)/shard_map/hyena_block/pallas_call | solution.py:465
  43.7 0.7 %copy.10 = bf16[256,512]{1,0:T(8,128)(2,1)} copy(bf16[256,512]{1,0:T(8,128)(2,1)S(1)} %hyena_block.1) | data formatting | bytes 524288

commit v5 on v4

--- a/solution.py
+++ b/solution.py
@@ -271,7 +271,6 @@
     seed = half(1 - y_hi, z, core)
     landed(seed, wr.at[1, 0])
     spread(1, seed)
-    pass_on(0, 1)
     extend(0)
     extend_from_halo(0)
     lax.fori_loop(0, tiles, query_tile, 0)
@@ -338,6 +337,7 @@
         y_im = s_re * h_im + s_im * h_re
         both = jnp.concatenate([y_re, y_im], axis=0)
         intra[j] = jnp.dot(inv[...], split_rows(both), preferred_element_type=F32)
+    pass_on(0, 1)
     pass_on(1, 1)
 
     own_part = jnp.logical_and(scans, core == 0)

time: 44.5 us -> 43.2 us (0.971)
  Pallas kernels: 43.7 us -> 42.4 us
    pallas_call x1, Pallas kernels: 43.7 us -> 42.4 us  [shards(): pl.pallas_call(kernel, out_shape=pltpu.VMEM((rows, out_weight.shape[1]),...]
where the time goes in v5:
time: 43.2 us; the launch traced here: 43.1 us
  Pallas kernels  42.4 us (98%)
  local copies, waits for them, and re-layouts  0.71 us (2%)
    pallas_call x1, Pallas kernels, shards(): pl.pallas_call(kernel, out_shape=pltpu.VMEM((rows, out_weight.shape[1]),...  42.4 us

profile of v5, /device:TPU:1, one launch (start us, length us, event | category | flops | bytes accessed | tf_op | source)
XLA Modules:
  0.0 43.1 jit_solution(5298661566127220687)
XLA Ops:
  0.0 42.4 %hyena_block.1 = bf16[256,512]{1,0:T(8,128)(2,1)S(1)} custom-call(bf16[3,256,512]{2,1,0:T(8,128)(2,1)} %proj_in.1, f32[3,7,512]{2,1,0:T(8,128)} %sf_in.1, f32[16,512]{1,0:T(8,128)} %res_in.1, f32[16,512]{1,0:T(8,128)} %dec_in.1, s32[16]{0:T(128)} %docs_in.1, bf16[128,512]{1,0:T(8,128)(2,1)} %w.1, bf16[256,384]{1,0:T(8,128)(2,1)} %constant.4.clone.fwd_in, ...), custom_call_target="tpu_custom_call" | custom-call | tf_op jit(solution)/shard_map/hyena_block/pallas_call | solution.py:465
  42.4 0.7 %copy.10 = bf16[256,512]{1,0:T(8,128)(2,1)} copy(bf16[256,512]{1,0:T(8,128)(2,1)S(1)} %hyena_block.1) | data formatting | bytes 524288

commit v6 on v5

--- a/solution.py
+++ b/solution.py
@@ -139,8 +139,9 @@
     def spread(plane, src):
         hi = hi_of[plane]
         dst = half(hi, z, core)
-        started(remote(src, dst, ws.at[plane, 1], wr.at[plane, 1 + core], ctx_of(y_hi, (z + 1) % 8, 0), q))
-        started(remote(src, dst, ws.at[plane, 2], wr.at[plane, 1 + core], ctx_of(y_hi, (z + 7) % 8, 1), q))
+        if plane == 0:
+            started(remote(src, dst, ws.at[plane, 1], wr.at[plane, 1 + core], ctx_of(y_hi, (z + 1) % 8, 0), q))
+            started(remote(src, dst, ws.at[plane, 2], wr.at[plane, 1 + core], ctx_of(y_hi, (z + 7) % 8, 1), q))
         started(remote(src, dst, ws.at[plane, 6], wr.at[plane, 6], ctx_of(y_hi, z, 1 - core), q))
 
     def landed(ref, sem):
@@ -151,7 +152,9 @@
         oz = (z - step * hop + 8) % 8
         whole = wbuf.at[hi, oz]
         mine = half(hi, oz, core)
-        if hop == 1:
+        if plane == 1 and hop == 1:
+            landed(whole, wr.at[plane, 1])
+        elif hop == 1:
             landed(half(hi, oz, 0), wr.at[plane, 1])
             landed(half(hi, oz, 1), wr.at[plane, 2])
         elif hop < 4:
@@ -162,6 +165,8 @@
             started(remote(whole, whole, ws.at[plane, 2 + hop], wr.at[plane, 2 + hop], ctx_of(y_hi, z_next, core), q))
         elif hop == 3:
             started(remote(mine, mine, ws.at[plane, 5], wr.at[plane, 5], ctx_of(y_hi, z_next, core), q))
+        if plane == 0 and hop == 1:
+            started(remote(whole, whole, ws.at[1, 1], wr.at[1, 1], ctx_of(1 - y_hi, z, core), q))
         part = whole if hop < 4 else mine
         started(remote(part, part, ws.at[plane, 6 + hop], wr.at[plane, 6 + hop], ctx_of(y_hi, z, 1 - core), q))
 
@@ -269,6 +274,7 @@
             remote(parts.at[i % 4], rx.at[p], out_send.at[i], out_recv.at[group], scanner(i), q).start()
 
     seed = half(1 - y_hi, z, core)
+    pass_on(0, 1)
     landed(seed, wr.at[1, 0])
     spread(1, seed)
     extend(0)
@@ -337,7 +343,7 @@
         y_im = s_re * h_im + s_im * h_re
         both = jnp.concatenate([y_re, y_im], axis=0)
         intra[j] = jnp.dot(inv[...], split_rows(both), preferred_element_type=F32)
-    pass_on(0, 1)
+    pass_on(0, 2)
     pass_on(1, 1)
 
     own_part = jnp.logical_and(scans, core == 0)
@@ -367,8 +373,10 @@
 
         lax.fori_loop(0, tiles, hidden_tile, 0)
 
+    spans = {0: (0, BLK), 1: (BLK, BLK), 2: (BLK, 80), 3: (BLK + 80, 48)}
+
     def piece(b, j):
-        return hbuf.at[b, pl.ds(j * BLK, BLK), :]
+        return hbuf.at[b, pl.ds(*spans[j]), :]
 
     def give(idx, b, j, to):
         started(remote(piece(b, j), piece(b, j), hs.at[idx], hr.at[idx], p, to))
@@ -384,26 +392,51 @@
     give(1, q, 1, q_right)
     give(2, q, 0, q_left)
     give(4, q, 0, q_y)
-    pass_on(0, 2)
+    pass_on(0, 3)
     pass_on(1, 2)
     took(0, q_left, 0)
     give(6, q_left, 0, q_right)
     give(8, q_left, 0, q_y)
     took(5, q_y, 1)
-    give(11, q_y, 1, q_left)
-    give(10, q_y, 1, q_right)
+    give(11, q_y, 2, q_left)
+    give(10, q_y, 2, q_right)
     took(3, q_right, 1)
     give(7, q_right, 1, q_left)
-    pass_on(0, 3)
+    give(15, q_right, 3, q_y)
+    pass_on(0, 4)
     took(2, q_right, 0)
     give(9, q_right, 0, q_y)
+    took(1, q_left, 1)
+    give(14, q_left, 3, q_y)
     pass_on(1, 3)
     took(8, q_yleft, 0)
     give(12, q_yleft, 0, q_right)
-    took(11, q_yright, 1)
-    give(13, q_yright, 1, q_left)
-    pass_on(0, 4)
+    took(11, q_yright, 2)
+    give(13, q_yright, 2, q_left)
+    took(15, q_yright, 3)
+    give(16, q_yright, 3, q_left)
     pass_on(1, 4)
+
+    n_early = len(sends) - 12
+    for copy in sends[:n_early]:
+        copy.wait_send()
+
+    def handed_out(i, carry):
+        @pl.when(scanner(i) != p)
+        def _():
+            landed(parts.at[i % 4], out_send.at[i])
+
+        return carry
+
+    lax.fori_loop(4 * group, 16, handed_out, 0)
+
+    @pl.when(scans)
+    def _():
+        for n in range(8):
+
+            @pl.when(8 * serves + n != p)
+            def _():
+                landed(back.at[n], back_send.at[n])
 
     for plane in range(2):
         hi = hi_of[plane]
@@ -426,37 +459,21 @@
                 total = part if total is None else total + part
             acc[:, cols] = total
 
-    took(1, q_left, 1)
     took(4, q_y, 0)
     project_all((q_y, q, q_right, q_left), True)
     took(6, q_opp, 0)
     took(7, q_opp, 1)
     took(9, q_yright, 0)
-    took(10, q_yleft, 1)
+    took(10, q_yleft, 2)
+    took(14, q_yleft, 3)
     project_all((q_opp, q_yright, q_yleft), False)
     took(12, q_yopp, 0)
-    took(13, q_yopp, 1)
+    took(13, q_yopp, 2)
+    took(16, q_yopp, 3)
     out[...] = (acc[...] + product(q_yopp)).astype(BF16)
 
-    for copy in sends:
+    for copy in sends[n_early:]:
         copy.wait_send()
-
-    def handed_out(i, carry):
-        @pl.when(scanner(i) != p)
-        def _():
-            landed(parts.at[i % 4], out_send.at[i])
-
-        return carry
-
-    lax.fori_loop(4 * group, 16, handed_out, 0)
-
-    @pl.when(scans)
-    def _():
-        for n in range(8):
-
-            @pl.when(8 * serves + n != p)
-            def _():
-                landed(back.at[n], back_send.at[n])
 
 
 def shards(fwd, inv, projected, short_filter, residues, decay_rates, doc_blocks, out_weight):
@@ -505,8 +522,8 @@
             pltpu.SemaphoreType.DMA((1,)),
             pltpu.SemaphoreType.DMA((2, 11)),
             pltpu.SemaphoreType.DMA((2, 11)),
-            pltpu.SemaphoreType.DMA((14,)),
-            pltpu.SemaphoreType.DMA((14,)),
+            pltpu.SemaphoreType.DMA((17,)),
+            pltpu.SemaphoreType.DMA((17,)),
         ],
         compiler_params=pltpu.CompilerParams(
             collective_id=0, has_side_effects=True, vmem_limit_bytes=60 * 1024 * 1024

time: 43.2 us -> 42.8 us (level)
  Pallas kernels: 42.4 us -> 41.8 us
    pallas_call x1, Pallas kernels: 42.4 us -> 41.8 us  [shards(): pl.pallas_call(kernel, out_shape=pltpu.VMEM((rows, out_weight.shape[1]),...]
where the time goes in v6:
time: 42.8 us; the launch traced here: 42.6 us
  Pallas kernels  41.8 us (98%)
  local copies, waits for them, and re-layouts  0.71 us (2%)
    pallas_call x1, Pallas kernels, shards(): pl.pallas_call(kernel, out_shape=pltpu.VMEM((rows, out_weight.shape[1]),...  41.8 us

profile of v6, /device:TPU:1, one launch (start us, length us, event | category | flops | bytes accessed | tf_op | source)
XLA Modules:
  0.0 42.6 jit_solution(13224842325909225607)
XLA Ops:
  0.0 41.8 %hyena_block.1 = bf16[256,512]{1,0:T(8,128)(2,1)S(1)} custom-call(bf16[3,256,512]{2,1,0:T(8,128)(2,1)} %proj_in.1, f32[3,7,512]{2,1,0:T(8,128)} %sf_in.1, f32[16,512]{1,0:T(8,128)} %res_in.1, f32[16,512]{1,0:T(8,128)} %dec_in.1, s32[16]{0:T(128)} %docs_in.1, bf16[128,512]{1,0:T(8,128)(2,1)} %w.1, bf16[256,384]{1,0:T(8,128)(2,1)} %constant.4.clone.fwd_in, ...), custom_call_target="tpu_custom_call" | custom-call | tf_op jit(solution)/shard_map/hyena_block/pallas_call | solution.py:482
  41.8 0.7 %copy.10 = bf16[256,512]{1,0:T(8,128)(2,1)} copy(bf16[256,512]{1,0:T(8,128)(2,1)S(1)} %hyena_block.1) | data formatting | bytes 524288

commit v7 on v6

--- a/solution.py
+++ b/solution.py
@@ -404,11 +404,11 @@
     give(7, q_right, 1, q_left)
     give(15, q_right, 3, q_y)
     pass_on(0, 4)
+    pass_on(1, 3)
     took(2, q_right, 0)
     give(9, q_right, 0, q_y)
     took(1, q_left, 1)
     give(14, q_left, 3, q_y)
-    pass_on(1, 3)
     took(8, q_yleft, 0)
     give(12, q_yleft, 0, q_right)
     took(11, q_yright, 2)

time: 42.8 us -> 42.3 us (0.988)
  no operation moved by 1% of the time
where the time goes in v7:
time: 42.3 us; the launch traced here: 42.2 us
  Pallas kernels  41.5 us (98%)
  local copies, waits for them, and re-layouts  0.71 us (2%)
    pallas_call x1, Pallas kernels, shards(): pl.pallas_call(kernel, out_shape=pltpu.VMEM((rows, out_weight.shape[1]),...  41.5 us

profile of v7, /device:TPU:1, one launch (start us, length us, event | category | flops | bytes accessed | tf_op | source)
XLA Modules:
  0.0 42.2 jit_solution(6501003147080647791)
XLA Ops:
  0.0 41.5 %hyena_block.1 = bf16[256,512]{1,0:T(8,128)(2,1)S(1)} custom-call(bf16[3,256,512]{2,1,0:T(8,128)(2,1)} %proj_in.1, f32[3,7,512]{2,1,0:T(8,128)} %sf_in.1, f32[16,512]{1,0:T(8,128)} %res_in.1, f32[16,512]{1,0:T(8,128)} %dec_in.1, s32[16]{0:T(128)} %docs_in.1, bf16[128,512]{1,0:T(8,128)(2,1)} %w.1, bf16[256,384]{1,0:T(8,128)(2,1)} %constant.4.clone.fwd_in, ...), custom_call_target="tpu_custom_call" | custom-call | tf_op jit(solution)/shard_map/hyena_block/pallas_call | solution.py:482
  41.5 0.7 %copy.10 = bf16[256,512]{1,0:T(8,128)(2,1)} copy(bf16[256,512]{1,0:T(8,128)(2,1)S(1)} %hyena_block.1) | data formatting | bytes 524288
